TPU v7x, 512 devices: a whole 4x4x16 slice. The times are simulated.
512 devices in a mesh: mic: 64 (over z, x), src: 8 (over y, core).
Axes of the slice: x: 4, y: 4, z: 16, core: 2. Of those that a mesh axis runs over, the one named last changes fastest.
Arguments:
- tensor_slab: bfloat16 [32, 4096, 8192], P(None, 'src', 'mic'), may hold values from -6 to 6
- observed_blocks: int32 [64, 64], P('src', 'mic'), may hold values 0 or 1
- mic_factor: float32 [8192, 256], P('mic'), may hold values from -40 to 40
- time_factor: float32 [32, 256], replicated, may hold values from -6 to 6
Outputs:
- source_out: float32 [4096, 256], P('src')
- mic_out: float32 [8192, 256], P('mic')
- time_out: float32 [32, 256], replicated
All inputs are finite; a program needn't handle non-finite values. No bound on the sum of `observed_blocks` on one device may be relied on, other than what follows from the above.
Results may differ from a plain program's by a relative error of at most 0.012.
Values sent between devices are 32-bit elements; how exact they have to be, the bound alone decides.
A program may use at most 64 MiB of HBM per device.

v0:
```python
import jax
import jax.numpy as jnp
from jax import lax
from jax.sharding import PartitionSpec as P

SRC_BLK = 64
MIC_BLK = 128


def expand_blocks(blocks):
    rows_blocks, cols_blocks = blocks.shape
    spread = jnp.broadcast_to(
        blocks[:, None, :, None], (rows_blocks, SRC_BLK, cols_blocks, MIC_BLK)
    )
    return spread.reshape(rows_blocks * SRC_BLK, cols_blocks * MIC_BLK).astype(jnp.bfloat16)


def gram_of(factor):
    return jnp.dot(
        factor.T, factor, precision=lax.Precision.HIGHEST, preferred_element_type=jnp.float32
    )


def normalize(raw, gram, count):
    scales = jnp.sqrt(jnp.diagonal(gram) / count + 1e-06)
    return (raw / scales[None, :], gram / (scales[:, None] * scales[None, :]))


def solve_rows(system, right):
    lower = jnp.linalg.cholesky(system)
    middle = lax.linalg.triangular_solve(
        lower, right, left_side=False, lower=True, transpose_a=True
    )
    return lax.linalg.triangular_solve(
        lower, middle, left_side=False, lower=True, transpose_a=False
    )


def khatri_rao(time_factor, low_rows):
    return (time_factor[:, None, :] * low_rows.astype(jnp.float32)[None, :, :]).astype(jnp.bfloat16)


def reduce_mic_gram(factor):
    return lax.psum(gram_of(factor), "mic")


def on_device(tensor_slab, observed_blocks, mic_factor, time_factor):
    keep = expand_blocks(observed_blocks)
    observed = tensor_slab * keep[None, :, :]
    samples, src_dev, mic_dev = observed.shape
    mic_count = lax.axis_size("mic")
    src_count = lax.axis_size("src")
    src_total = src_dev * src_count
    mic_total = mic_dev * mic_count
    gram_time = gram_of(time_factor)
    mic_low = mic_factor.astype(jnp.bfloat16)
    kr_mic = khatri_rao(time_factor, mic_low)
    system_src = reduce_mic_gram(mic_factor) * gram_time / (mic_total * samples)
    piece = observed
    source_mttkrp = lax.psum(
        jnp.einsum("ksm,kmr->sr", piece, kr_mic, preferred_element_type=jnp.float32), "mic"
    )
    source_raw = solve_rows(system_src, source_mttkrp)
    gram_src_raw = lax.psum(gram_of(source_raw), "src")
    source_out, gram_src = normalize(source_raw, gram_src_raw, src_total)
    src_low = source_out.astype(jnp.bfloat16)
    kr_src = khatri_rao(time_factor, src_low)
    system_mic = gram_src * gram_time / (src_total * samples)
    piece = observed
    mic_mttkrp = lax.psum(
        jnp.einsum("ksm,ksr->mr", piece, kr_src, preferred_element_type=jnp.float32), "src"
    )
    mic_raw = solve_rows(system_mic, mic_mttkrp)
    gram_mic_raw = reduce_mic_gram(mic_raw)
    mic_out, gram_mic = normalize(mic_raw, gram_mic_raw, mic_total)
    mic_new_low = mic_out.astype(jnp.bfloat16)
    inner = jnp.einsum("ksm,mr->ksr", observed, mic_new_low, preferred_element_type=jnp.float32)
    time_term = jnp.sum(inner * source_out[None, :, :], axis=1)
    time_mttkrp = lax.psum(time_term, ("mic", "src"))
    system_time = gram_src * gram_mic / (src_total * mic_total)
    time_raw = solve_rows(system_time, time_mttkrp)
    time_out, _ = normalize(time_raw, gram_of(time_raw), samples)
    return (source_out, mic_out, time_out)


def solution(mesh):
    placed = (P(None, "src", "mic"), P("src", "mic"), P("mic", None), P())
    return jax.shard_map(
        on_device,
        mesh=mesh,
        in_specs=placed,
        out_specs=(P("src", None), P("mic", None), P()),
        check_vma=False,
    )
```

profile of v0, /device:TPU:1, one launch (start us, length us, event | category | flops | bytes accessed | tf_op | source)
XLA Modules:
  0.0 955.7 jit_solution(13764541191049478510)
XLA Ops:
  11.1 4.3 fusion.12
  15.4 264.4 %all-reduce.13.cloned.1.call-done = (f32[512,256]{1,0:T(8,128)}, f32[256,256]{0,1:T(8,128)}) async-done(((f32[512,256]{1,0:T(8,128)}, f32[256,256]{0,1:T(8,128)}), (f32[512,256]{1,0:T(8,128)}, f32[256,256]{0,1:T(8,128)})) %all-reduce.13.cloned.1.call-update) | async-done | bytes 786448 | tf_op jit(solution)/shard_map/psum | solution.py:60
  281.4 11.7 %cholesky.172 = f32[128,128]{1,0:T(8,128)S(1)} custom-call(f32[128,128]{1,0:T(8,128)S(1)} %cholesky.270), custom_call_target="Cholesky" | custom-call | tf_op jit(solution)/shard_map/jit(cholesky)/cholesky | solution.py:30
  293.2 9.8 %custom-call.34 = f32[1,128,128]{1,2,0:T(8,128)S(1)} custom-call(f32[1,128,128]{2,1,0:T(8,128)S(1)} %get-tuple-element.79), custom_call_target="InvertDiagBlocksLowerTriangular" | custom-call | tf_op jit(solution)/shard_map/jit(cholesky)/cholesky | solution.py:30
  303.5 11.7 %cholesky.189 = f32[128,128]{1,0:T(8,128)S(1)} custom-call(f32[128,128]{1,0:T(8,128)S(1)} %convolution_subtract_fusion.6), custom_call_target="Cholesky" | custom-call | tf_op jit(solution)/shard_map/jit(cholesky)/cholesky | solution.py:30
  317.4 4.3 while.3
  321.7 19.7 %custom-call.23 = f32[2,128,128]{1,2,0:T(8,128)S(1)} custom-call(f32[2,128,128]{2,1,0:T(8,128)S(1)} %get-tuple-element.11), custom_call_target="InvertDiagBlocksLowerTriangular" | custom-call | tf_op jit(solution)/shard_map/triangular_solve | solution.py:31
  345.3 79.1 %all-reduce.7.cloned.1.call-done = f32[256,256]{0,1:T(8,128)} async-done(((f32[256,256]{0,1:T(8,128)}), f32[256,256]{0,1:T(8,128)}) %all-reduce.7.cloned.1.call-update) | async-done | bytes 262160 | tf_op jit(solution)/shard_map/psum | solution.py:64
  424.4 2.6 gather_fusion
  427.4 5.1 fusion.15
  433.1 11.7 %cholesky.206 = f32[128,128]{1,0:T(8,128)S(1)} custom-call(f32[128,128]{1,0:T(8,128)S(1)} %cholesky.273), custom_call_target="Cholesky" | custom-call | tf_op jit(solution)/shard_map/jit(cholesky)/cholesky | solution.py:30
  444.9 9.8 %custom-call.35 = f32[1,128,128]{1,2,0:T(8,128)S(1)} custom-call(f32[1,128,128]{2,1,0:T(8,128)S(1)} %get-tuple-element.75), custom_call_target="InvertDiagBlocksLowerTriangular" | custom-call | tf_op jit(solution)/shard_map/jit(cholesky)/cholesky | solution.py:30
  455.2 11.7 %cholesky.223 = f32[128,128]{1,0:T(8,128)S(1)} custom-call(f32[128,128]{1,0:T(8,128)S(1)} %convolution_subtract_fusion.5), custom_call_target="Cholesky" | custom-call | tf_op jit(solution)/shard_map/jit(cholesky)/cholesky | solution.py:30
  469.7 4.1 while.4
  473.8 20.1 %custom-call.24 = f32[2,128,128]{1,2,0:T(8,128)S(1)} custom-call(f32[2,128,128]{2,1,0:T(8,128)S(1)} %get-tuple-element.19), custom_call_target="InvertDiagBlocksLowerTriangular" | custom-call | tf_op jit(solution)/shard_map/triangular_solve | solution.py:31
  493.9 13.2 %all-reduce.9.cloned.1.call-done = f32[128,256]{1,0:T(8,128)} async-done(((f32[128,256]{1,0:T(8,128)}), f32[128,256]{1,0:T(8,128)}) %all-reduce.9.cloned.1.call-update) | async-done | bytes 131088 | tf_op jit(solution)/shard_map/psum | solution.py:70
  511.6 253.2 %all-reduce.11.cloned.1.call-done = f32[256,256]{0,1:T(8,128)} async-done(((f32[256,256]{0,1:T(8,128)}), f32[256,256]{0,1:T(8,128)}) %all-reduce.11.cloned.1.call-update) | async-done | bytes 262160 | tf_op jit(solution)/shard_map/psum | solution.py:44
  769.6 11.7 %cholesky.240 = f32[128,128]{1,0:T(8,128)S(1)} custom-call(f32[128,128]{1,0:T(8,128)S(1)} %cholesky.276), custom_call_target="Cholesky" | custom-call | tf_op jit(solution)/shard_map/jit(cholesky)/cholesky | solution.py:30
  781.4 9.8 %custom-call.36 = f32[1,128,128]{1,2,0:T(8,128)S(1)} custom-call(f32[1,128,128]{2,1,0:T(8,128)S(1)} %get-tuple-element.71), custom_call_target="InvertDiagBlocksLowerTriangular" | custom-call | tf_op jit(solution)/shard_map/jit(cholesky)/cholesky | solution.py:30
  791.7 11.9 %cholesky.257 = f32[128,128]{1,0:T(8,128)S(1)} custom-call(f32[128,128]{1,0:T(8,128)S(1)} %convolution_subtract_fusion.2), custom_call_target="Cholesky" | custom-call | tf_op jit(solution)/shard_map/jit(cholesky)/cholesky | solution.py:30
  806.2 4.1 while.5
  810.3 19.7 %custom-call.25 = f32[2,128,128]{1,2,0:T(8,128)S(1)} custom-call(f32[2,128,128]{2,1,0:T(8,128)S(1)} %get-tuple-element.27), custom_call_target="InvertDiagBlocksLowerTriangular" | custom-call | tf_op jit(solution)/shard_map/triangular_solve | solution.py:31
  830.0 4.6 multiply_reduce_fusion
  834.7 109.8 %psum.47 = f32[32,256]{1,0:T(8,128)S(1)} all-reduce(f32[32,256]{1,0:T(8,128)S(1)} %multiply_reduce_fusion), channel_id=1, replica_groups=mesh['mic'=64,'src'=8] {'mic','src'}, use_global_device_ids=true, to_apply=%region_10.12 | all-reduce | flops 8192 | bytes 65536 | tf_op jit(solution)/shard_map/psum | solution.py:79
  (112 shorter events, 41.5 us)
Async XLA Ops:
  7.2 272.6 %all-reduce.13.cloned.1.call-start = ((), (), s32[]{:S(2)}) async-start(), calls=%async_computation.3 | async-start | bytes 1572864 | tf_op jit(solution)/shard_map/psum | solution.py:60
  11.1 268.8 %copy-start.3 = (f32[32,256]{1,0:T(8,128)S(1)}, f32[32,256]{1,0:T(8,128)}, u32[]{:S(2)}) copy-start(f32[32,256]{1,0:T(8,128)} %param.8) | copy-start | bytes 98308
  15.4 409.1 %all-reduce.7.cloned.1.call-start = ((), (), s32[]{:S(2)}) async-start(), calls=%async_computation | async-start | bytes 524288 | tf_op jit(solution)/shard_map/psum | solution.py:64
  279.8 61.6 %copy-start.2 = (f32[512,256]{1,0:T(8,128)S(1)}, f32[512,256]{1,0:T(8,128)}, u32[]{:S(2)}) copy-start(f32[512,256]{1,0:T(8,128)} %get-tuple-element.58) | copy-start | bytes 1572868
  345.3 161.8 %all-reduce.9.cloned.1.call-start = ((), (), s32[]{:S(2)}) async-start(), calls=%async_computation.1 | async-start | bytes 262144 | tf_op jit(solution)/shard_map/psum | solution.py:70
  427.4 5.4 copy-start
  432.5 332.3 %all-reduce.11.cloned.1.call-start = ((), (), s32[]{:S(2)}) async-start(), calls=%async_computation.2 | async-start | bytes 524288 | tf_op jit(solution)/shard_map/psum | solution.py:44
  511.6 323.1 %copy-start.1 = (f32[512,256]{1,0:T(8,128)}, f32[512,256]{1,0:T(8,128)S(1)}, u32[]{:S(2)}) copy-start(f32[512,256]{1,0:T(8,128)S(1)} %copy.33) | copy-start | bytes 1572868
Sparse Core Ops, SparseCore 0:
  15.5 264.2 all-reduce.12
  345.4 78.9 all-reduce.6
  432.7 74.3 all-reduce.8
  511.5 253.2 all-reduce.10
where the time goes:
time: 965 us; the launch traced here: 956 us
  waiting for transfers between devices  610 us (63%)
  other arithmetic  167 us (17%)
  blocking collectives  110 us (11%)
  matrix products  28.6 us (3%)
  local copies, waits for them, and re-layouts  21.6 us (2%)
  between operations  18.4 us (2%)
    psum x1, waiting for transfers between devices, on_device(): lax.psum(jnp.einsum('ksm,kmr->sr', piece, kr_mic, preferred_element_type=...  264 us
    psum x1, waiting for transfers between devices, reduce_mic_gram(): return lax.psum(gram_of(factor), 'mic')  253 us
    psum x1, blocking collectives, on_device(): time_mttkrp = lax.psum(time_term, ('mic', 'src'))  110 us
    another operation x20, other arithmetic, solve_rows(): lower = jnp.linalg.cholesky(system)  103 us
    psum x1, waiting for transfers between devices, on_device(): gram_src_raw = lax.psum(gram_of(source_raw), 'src')  79.1 us
    another operation x7, other arithmetic, solve_rows(): lax.linalg.triangular_solve(lower, right, left_side=False, lower=True, tr...  59.5 us
  transfers between devices with their start and end apart: 4, of which 4 were waited for; matrix products, arithmetic and copies ran while one was open for 6% of the time, Pallas kernels for 0%

commit v1 on v0

v1 whole, which is shorter than its diff:
```python
import functools

import jax
import jax.numpy as jnp
from jax import lax
from jax.experimental import pallas as pl
from jax.experimental.pallas import tpu as pltpu
from jax.sharding import PartitionSpec as P

MESH = pl.DeviceIdType.MESH
F32 = jnp.float32
BF16 = jnp.bfloat16

RANK = 256
SAMPLES = 32
SRC_DEV = 512
MIC_DEV = 128
SRC_BLK = 64
NX = 4
NZ = 16
NSRC = 8
NXS = NX * NSRC
SRC_ALL = SRC_DEV * NSRC
MIC_ALL = MIC_DEV * NX * NZ
BLK = 32


def exact_dot(a, b, dims=((1,), (0,))):
    return lax.dot_general(
        a, b, (dims, ((), ())), precision=lax.Precision.HIGHEST, preferred_element_type=F32
    )


def split3(a):
    first = a.astype(BF16)
    rest = a - first.astype(F32)
    second = rest.astype(BF16)
    third = (rest - second.astype(F32)).astype(BF16)
    return first, second, third


def outer_dot(a, b):
    a0, a1, a2 = split3(a)
    b0, b1, b2 = split3(b)
    left = jnp.concatenate([a0, a0, a1, a1, a0, a2], axis=0)
    right = jnp.concatenate([b0, b1, b0, b1, b2, b0], axis=0)
    return lax.dot_general(left, right, (((0,), (0,)), ((), ())), preferred_element_type=F32)


def invert(a_ref):
    lane = lax.broadcasted_iota(jnp.int32, (BLK, RANK), 1)
    sub = lax.broadcasted_iota(jnp.int32, (BLK, RANK), 0)
    lane_row = lax.broadcasted_iota(jnp.int32, (1, RANK), 1)

    def block(i, carry):
        base = pl.multiple_of(i * BLK, BLK)
        old = a_ref[pl.ds(base, BLK), :]
        panel = pltpu.roll(old, RANK - base, 1)
        for j in range(BLK):
            column = panel[:, j : j + 1]
            inv = 1.0 / panel[j : j + 1, j : j + 1]
            row = jnp.where(lane_row == j, inv, panel[j : j + 1, :] * inv)
            other = jnp.where(lane == j, 0.0, panel) - column * row
            panel = jnp.where(sub == j, row, other)
        panel = pltpu.roll(panel, base, 1)
        inside = (lane_row >= base) & (lane_row < base + BLK)
        column = jnp.where(lane < base, -old, old)
        update = outer_dot(column, panel)
        a_ref[...] = jnp.where(inside, 0.0, a_ref[...]) - update
        a_ref[pl.ds(base, BLK), :] = panel
        return carry

    lax.fori_loop(0, RANK // BLK, block, 0)


def diagonal(gram):
    rows = lax.broadcasted_iota(jnp.int32, (RANK, RANK), 0)
    cols = lax.broadcasted_iota(jnp.int32, (RANK, RANK), 1)
    only = jnp.where(rows == cols, gram, 0.0)
    return jnp.sum(only, axis=0, keepdims=True), jnp.sum(only, axis=1, keepdims=True)


def scales_of(gram, count):
    row, col = diagonal(gram)
    return jnp.sqrt(row / count + 1e-06), jnp.sqrt(col / count + 1e-06)


def drain(ref, sem):
    pltpu.make_async_copy(ref, ref, sem).wait()


def kernel(
    x_hbm,
    blk_ref,
    mic_ref,
    time_ref,
    src_out,
    mic_out,
    time_out,
    x_v,
    xt_v,
    kr_v,
    p_v,
    y_v,
    yx_v,
    y128_v,
    yz_v,
    raw8_v,
    raw_v,
    low_v,
    gram_v,
    g2_v,
    g3_v,
    gn_v,
    gx_v,
    gz_v,
    g8_v,
    gram1_v,
    a_v,
    gt_v,
    gs_v,
    gs8_v,
    gram2_v,
    mm_v,
    mr_v,
    mraw_v,
    t_v,
    tr_v,
    hx_v,
    h_v,
    hz_v,
    h2_v,
    hy_v,
    h3_v,
    gram3_v,
    load_sem,
    send_sem,
    recv_sem,
):
    me_mic = lax.axis_index("mic")
    src = lax.axis_index("src")
    z = me_mic // NX
    x = me_mic % NX
    p = x * NSRC + src

    def at(zz, xx, ss):
        return (zz * NX + xx, ss)

    load = pltpu.make_async_copy(x_hbm, x_v, load_sem)
    load.start()

    barrier = pltpu.get_barrier_semaphore()

    def greet_z(d, c):
        pl.semaphore_signal(barrier, inc=1, device_id=at((z + d) % NZ, x, src), device_id_type=MESH)
        return c

    def greet_xs(d, c):
        q = (p + d) % NXS
        pl.semaphore_signal(
            barrier, inc=1, device_id=at(z, q // NSRC, q % NSRC), device_id_type=MESH
        )
        return c

    lax.fori_loop(1, NZ, greet_z, 0)
    lax.fori_loop(1, NXS, greet_xs, 0)

    def send(src_ref, dst_ref, stage, device):
        pltpu.make_async_remote_copy(
            src_ref=src_ref,
            dst_ref=dst_ref,
            send_sem=send_sem.at[stage],
            recv_sem=recv_sem.at[stage],
            device_id=device,
            device_id_type=MESH,
        ).start()

    def gather_xs(piece_ref, full_ref, stage):
        def one(d, c):
            q = (p + d) % NXS
            send(piece_ref, full_ref.at[p], stage, at(z, q // NSRC, q % NSRC))
            return c

        lax.fori_loop(1, NXS, one, 0)

    mic = mic_ref[...]
    gram_v[...] = exact_dot(mic, mic, ((0,), (0,)))
    times = time_ref[...]
    gt_v[...] = exact_dot(times, times, ((0,), (0,)))
    mic_low = mic.astype(BF16).astype(F32)

    def make_kr(k, c):
        kr_v[pl.ds(pl.multiple_of(k * MIC_DEV, MIC_DEV), MIC_DEV), :] = (
            time_ref[pl.ds(k, 1), :] * mic_low
        ).astype(BF16)
        return c

    lax.fori_loop(0, SAMPLES, make_kr, 0)

    pl.semaphore_wait(barrier, NZ - 1 + NXS - 1)

    def gram_x(gram_ref, dst, stage):
        def one(d, c):
            xx = (x + d) % NX
            rows = pl.ds(pl.multiple_of(xx * 64 + src * 8, 8), 8)
            send(gram_ref.at[rows, :], dst.at[x], stage, at(z, xx, src))
            return c

        lax.fori_loop(1, NX, one, 0)

    own_rows = pl.ds(pl.multiple_of(x * 64 + src * 8, 8), 8)
    gram_x(gram_v, gx_v, 0)
    gx_v[x] = gram_v[own_rows, :]

    load.wait()

    def chunk(d, c):
        xx = (x + d) % NX
        start = xx * 128

        def part(kk, acc):
            left = jnp.concatenate(
                [x_v[kk * 8 + i, pl.ds(pl.multiple_of(start, 128), 128), :] for i in range(8)],
                axis=1,
            )
            right = kr_v[pl.ds(pl.multiple_of(kk * 1024, 1024), 1024), :]
            return acc + jnp.dot(left, right, preferred_element_type=F32)

        acc = lax.fori_loop(0, SAMPLES // 8, part, jnp.zeros((128, RANK), F32))
        for h in range(2):
            keep = blk_ref[xx * 2 + h, 0].astype(F32)
            y_v[pl.ds(pl.multiple_of(start + h * 64, 64), 64), :] = (
                acc[h * 64 : (h + 1) * 64, :] * keep
            )
        return c

    def chunk_send(d, c):
        chunk(d, c)
        xx = (x + d) % NX
        rows = pl.ds(pl.multiple_of(xx * 128, 128), 128)
        send(y_v.at[rows, :], yx_v.at[x], 1, at(z, xx, src))
        return c

    lax.fori_loop(1, NX, chunk_send, 0)
    chunk(0, 0)

    drain(gx_v.at[pl.ds(0, NX - 1)], recv_sem.at[0])
    g8_v[...] = (gx_v[0] + gx_v[1]) + (gx_v[2] + gx_v[3])

    def gram_z(d, c):
        zz = (z + d) % NZ
        send(g8_v, gz_v.at[z], 2, at(zz, x, src))
        return c

    lax.fori_loop(1, NZ, gram_z, 0)
    gz_v[z] = g8_v[...]

    yx_v[x] = y_v[pl.ds(pl.multiple_of(x * 128, 128), 128), :]
    drain(yx_v.at[pl.ds(0, NX - 1)], recv_sem.at[1])
    y128_v[...] = (yx_v[0] + yx_v[1]) + (yx_v[2] + yx_v[3])

    def rows_z(d, c):
        zz = (z + d) % NZ
        send(y128_v.at[pl.ds(pl.multiple_of(zz * 8, 8), 8), :], yz_v.at[z], 3, at(zz, x, src))
        return c

    lax.fori_loop(1, NZ, rows_z, 0)
    yz_v[z] = y128_v[pl.ds(pl.multiple_of(z * 8, 8), 8), :]

    drain(gz_v.at[pl.ds(0, NZ - 1)], recv_sem.at[2])
    raw8_v[...] = jnp.sum(gz_v[...], axis=0)
    gather_xs(raw8_v, gram1_v, 4)
    gram1_v[p] = raw8_v[...]

    def flip(k, c):
        xt_v[k] = x_v[k].T
        return c

    lax.fori_loop(0, SAMPLES, flip, 0)

    drain(gram1_v.at[pl.ds(0, NXS - 1)], recv_sem.at[4])
    a_v[...] = gram1_v[...].reshape(RANK, RANK) * gt_v[...] / (MIC_ALL * SAMPLES)
    invert(a_v)

    drain(yz_v.at[pl.ds(0, NZ - 1)], recv_sem.at[3])
    solved = exact_dot(jnp.sum(yz_v[...], axis=0), a_v[...])
    mine = pl.ds(pl.multiple_of(x * 128 + z * 8, 8), 8)
    raw_v[mine, :] = solved

    def back_z(d, c):
        zz = (z + d) % NZ
        send(raw_v.at[mine, :], raw_v.at[mine, :], 5, at(zz, x, src))
        return c

    lax.fori_loop(1, NZ, back_z, 0)
    drain(raw_v.at[pl.ds(0, 8 * (NZ - 1)), :], recv_sem.at[5])
    band = pl.ds(pl.multiple_of(x * 128, 128), 128)

    def back_x(d, c):
        xx = (x + d) % NX
        send(raw_v.at[band, :], raw_v.at[band, :], 6, at(z, xx, src))
        return c

    lax.fori_loop(1, NX, back_x, 0)
    drain(raw_v.at[pl.ds(0, 128 * (NX - 1)), :], recv_sem.at[6])

    raw = raw_v[...]
    gram2 = exact_dot(raw, raw, ((0,), (0,)))
    g2_v[...] = gram2

    def gram_s(d, c):
        ss = (src + d) % NSRC
        rows = pl.ds(pl.multiple_of(x * 64 + ss * 8, 8), 8)
        send(g2_v.at[rows, :], gs_v.at[src], 7, at(z, x, ss))
        return c

    lax.fori_loop(1, NSRC, gram_s, 0)
    gs_v[src] = g2_v[own_rows, :]

    for b in range(SRC_DEV // SRC_BLK):
        keep = blk_ref[b, 0].astype(F32)
        low_v[b * SRC_BLK : (b + 1) * SRC_BLK, :] = (
            raw_v[b * SRC_BLK : (b + 1) * SRC_BLK, :] * keep
        ).astype(BF16)

    def mic_part(kk, acc):
        low = low_v[...]
        left = xt_v[pl.ds(kk * 4, 4)].reshape(4 * MIC_DEV, SRC_DEV)
        prod = jnp.dot(left, low, preferred_element_type=F32)
        for i in range(4):
            piece = prod[i * MIC_DEV : (i + 1) * MIC_DEV, :]
            p_v[kk * 4 + i] = piece
            acc = acc + time_ref[pl.ds(kk * 4 + i, 1), :] * piece
        return acc

    mm_v[...] = lax.fori_loop(0, SAMPLES // 4, mic_part, jnp.zeros((MIC_DEV, RANK), F32))

    def mm_s(d, c):
        ss = (src + d) % NSRC
        rows = pl.ds(pl.multiple_of(ss * 16, 16), 16)
        send(mm_v.at[rows, :], mr_v.at[src], 8, at(z, x, ss))
        return c

    lax.fori_loop(1, NSRC, mm_s, 0)
    mic_rows = pl.ds(pl.multiple_of(src * 16, 16), 16)
    mr_v[src] = mm_v[mic_rows, :]

    drain(gs_v.at[pl.ds(0, NSRC - 1)], recv_sem.at[7])
    gs8_v[...] = jnp.sum(gs_v[...], axis=0)
    gather_xs(gs8_v, gram2_v, 9)
    gram2_v[p] = gs8_v[...]
    drain(gram2_v.at[pl.ds(0, NXS - 1)], recv_sem.at[9])
    gram_src = gram2_v[...].reshape(RANK, RANK)
    src_row, src_col = scales_of(gram_src, SRC_ALL)
    gram_src = gram_src / (src_row * src_col)
    gn_v[...] = gram_src
    a_v[...] = gram_src * gt_v[...] / (SRC_ALL * SAMPLES)
    src_out[...] = raw_v[...] / src_row
    invert(a_v)
    drain(mr_v.at[pl.ds(0, NSRC - 1)], recv_sem.at[8])
    right = jnp.sum(mr_v[...], axis=0) / src_row
    mraw_v[mic_rows, :] = exact_dot(right, a_v[...])

    def back_s(d, c):
        ss = (src + d) % NSRC
        send(mraw_v.at[mic_rows, :], mraw_v.at[mic_rows, :], 10, at(z, x, ss))
        return c

    lax.fori_loop(1, NSRC, back_s, 0)
    drain(mraw_v.at[pl.ds(0, 16 * (NSRC - 1)), :], recv_sem.at[10])

    mraw = mraw_v[...]
    g3_v[...] = exact_dot(mraw, mraw, ((0,), (0,)))

    def gram_x2(d, c):
        xx = (x + d) % NX
        rows = pl.ds(pl.multiple_of(xx * 64 + src * 8, 8), 8)
        send(g3_v.at[rows, :], hx_v.at[x], 11, at(z, xx, src))
        return c

    lax.fori_loop(1, NX, gram_x2, 0)
    hx_v[x] = g3_v[own_rows, :]

    def time_part(kb, c):
        rows = [
            jnp.sum(p_v[kb * 8 + i] * mraw_v[...], axis=0, keepdims=True) for i in range(8)
        ]
        piece = jnp.concatenate(rows, axis=0)
        t_v[kb] = piece[:, :128]
        t_v[kb + 4] = piece[:, 128:]
        return c

    lax.fori_loop(0, SAMPLES // 8, time_part, 0)

    def time_s(d, c):
        ss = (src + d) % NSRC
        send(t_v.at[ss], tr_v.at[src], 12, at(z, x, ss))
        return c

    lax.fori_loop(1, NSRC, time_s, 0)
    tr_v[src] = t_v[src]

    drain(hx_v.at[pl.ds(0, NX - 1)], recv_sem.at[11])
    drain(tr_v.at[pl.ds(0, NSRC - 1)], recv_sem.at[12])
    h_v[:, :RANK] = (hx_v[0] + hx_v[1]) + (hx_v[2] + hx_v[3])
    h_v[:, RANK:] = jnp.sum(tr_v[...], axis=0)

    zlo = z % 4
    zhi = z // 4

    def near(d, c):
        zz = zhi * 4 + (zlo + d) % 4
        send(h_v, hz_v.at[zlo], 13, at(zz, x, src))
        return c

    lax.fori_loop(1, 4, near, 0)
    hz_v[zlo] = h_v[...]
    drain(hz_v.at[pl.ds(0, 3)], recv_sem.at[13])
    h2_v[...] = (hz_v[0] + hz_v[1]) + (hz_v[2] + hz_v[3])

    def far(d, c):
        zz = ((zhi + d) % 4) * 4 + zlo
        send(h2_v, hy_v.at[zhi], 14, at(zz, x, src))
        return c

    lax.fori_loop(1, 4, far, 0)
    hy_v[zhi] = h2_v[...]
    drain(hy_v.at[pl.ds(0, 3)], recv_sem.at[14])
    h3_v[...] = (hy_v[0] + hy_v[1]) + (hy_v[2] + hy_v[3])
    gather_xs(h3_v, gram3_v, 15)
    gram3_v[p] = h3_v[...]
    drain(gram3_v.at[pl.ds(0, NXS - 1)], recv_sem.at[15])

    gram_mic = gram3_v[:, :, :RANK].reshape(RANK, RANK)
    mic_row, mic_col = scales_of(gram_mic, MIC_ALL)
    a_v[...] = gn_v[...] * (gram_mic / (mic_row * mic_col)) / (SRC_ALL * MIC_ALL)
    mic_out[...] = mraw_v[...] / mic_row
    invert(a_v)

    pieces = gram3_v[:, :, RANK:]
    parts = []
    for j in range(NSRC):
        parts.append((pieces[j] + pieces[8 + j]) + (pieces[16 + j] + pieces[24 + j]))
    total = jnp.concatenate(
        [jnp.concatenate([parts[kb], parts[kb + 4]], axis=1) for kb in range(4)], axis=0
    )
    total = total / (src_row * mic_row)
    time_raw = exact_dot(total, a_v[...])
    time_diag = jnp.sum(time_raw * time_raw, axis=0, keepdims=True)
    time_out[...] = time_raw / jnp.sqrt(time_diag / SAMPLES + 1e-06)

    drain(gx_v.at[pl.ds(0, NX - 1)], send_sem.at[0])
    drain(yx_v.at[pl.ds(0, NX - 1)], send_sem.at[1])
    drain(gz_v.at[pl.ds(0, NZ - 1)], send_sem.at[2])
    drain(yz_v.at[pl.ds(0, NZ - 1)], send_sem.at[3])
    drain(gram1_v.at[pl.ds(0, NXS - 1)], send_sem.at[4])
    drain(raw_v.at[pl.ds(0, 8 * (NZ - 1)), :], send_sem.at[5])
    drain(raw_v.at[pl.ds(0, 128 * (NX - 1)), :], send_sem.at[6])
    drain(gs_v.at[pl.ds(0, NSRC - 1)], send_sem.at[7])
    drain(mr_v.at[pl.ds(0, NSRC - 1)], send_sem.at[8])
    drain(gram2_v.at[pl.ds(0, NXS - 1)], send_sem.at[9])
    drain(mraw_v.at[pl.ds(0, 16 * (NSRC - 1)), :], send_sem.at[10])
    drain(hx_v.at[pl.ds(0, NX - 1)], send_sem.at[11])
    drain(tr_v.at[pl.ds(0, NSRC - 1)], send_sem.at[12])
    drain(hz_v.at[pl.ds(0, 3)], send_sem.at[13])
    drain(hy_v.at[pl.ds(0, 3)], send_sem.at[14])
    drain(gram3_v.at[pl.ds(0, NXS - 1)], send_sem.at[15])


def on_device(tensor_slab, observed_blocks, mic_factor, time_factor):
    vmem = pl.BlockSpec(memory_space=pltpu.VMEM)
    return pl.pallas_call(
        kernel,
        out_shape=(
            jax.ShapeDtypeStruct((SRC_DEV, RANK), F32),
            jax.ShapeDtypeStruct((MIC_DEV, RANK), F32),
            jax.ShapeDtypeStruct((SAMPLES, RANK), F32),
        ),
        in_specs=[
            pl.BlockSpec(memory_space=pl.ANY),
            pl.BlockSpec(memory_space=pltpu.SMEM),
            vmem,
            vmem,
        ],
        out_specs=(vmem, vmem, vmem),
        scratch_shapes=[
            pltpu.VMEM((SAMPLES, SRC_DEV, MIC_DEV), BF16),
            pltpu.VMEM((SAMPLES, MIC_DEV, SRC_DEV), BF16),
            pltpu.VMEM((SAMPLES * MIC_DEV, RANK), BF16),
            pltpu.VMEM((SAMPLES, MIC_DEV, RANK), F32),
            pltpu.VMEM((SRC_DEV, RANK), F32),
            pltpu.VMEM((NX, 128, RANK), F32),
            pltpu.VMEM((128, RANK), F32),
            pltpu.VMEM((NZ, 8, RANK), F32),
            pltpu.VMEM((8, RANK), F32),
            pltpu.VMEM((SRC_DEV, RANK), F32),
            pltpu.VMEM((SRC_DEV, RANK), BF16),
            pltpu.VMEM((RANK, RANK), F32),
            pltpu.VMEM((RANK, RANK), F32),
            pltpu.VMEM((RANK, RANK), F32),
            pltpu.VMEM((RANK, RANK), F32),
            pltpu.VMEM((NX, 8, RANK), F32),
            pltpu.VMEM((NZ, 8, RANK), F32),
            pltpu.VMEM((8, RANK), F32),
            pltpu.VMEM((NXS, 8, RANK), F32),
            pltpu.VMEM((RANK, RANK), F32),
            pltpu.VMEM((RANK, RANK), F32),
            pltpu.VMEM((NSRC, 8, RANK), F32),
            pltpu.VMEM((8, RANK), F32),
            pltpu.VMEM((NXS, 8, RANK), F32),
            pltpu.VMEM((MIC_DEV, RANK), F32),
            pltpu.VMEM((NSRC, 16, RANK), F32),
            pltpu.VMEM((MIC_DEV, RANK), F32),
            pltpu.VMEM((NSRC, 8, 128), F32),
            pltpu.VMEM((NSRC, 8, 128), F32),
            pltpu.VMEM((NX, 8, RANK), F32),
            pltpu.VMEM((8, RANK + 128), F32),
            pltpu.VMEM((4, 8, RANK + 128), F32),
            pltpu.VMEM((8, RANK + 128), F32),
            pltpu.VMEM((4, 8, RANK + 128), F32),
            pltpu.VMEM((8, RANK + 128), F32),
            pltpu.VMEM((NXS, 8, RANK + 128), F32),
            pltpu.SemaphoreType.DMA,
            pltpu.SemaphoreType.DMA((16,)),
            pltpu.SemaphoreType.DMA((16,)),
        ],
        compiler_params=pltpu.CompilerParams(
            collective_id=0, has_side_effects=True, vmem_limit_bytes=48 * 1024 * 1024
        ),
    )(tensor_slab, observed_blocks, mic_factor, time_factor)


def solution(mesh):
    placed = (P(None, "src", "mic"), P("src", "mic"), P("mic", None), P())
    return jax.shard_map(
        on_device,
        mesh=mesh,
        in_specs=placed,
        out_specs=(P("src", None), P("mic", None), P()),
        check_vma=False,
    )
```

time: 965 us -> 173 us (0.18)
  waiting for transfers between devices: 610 us -> 0 us
  other arithmetic: 167 us -> 0 us
  Pallas kernels: 0 us -> 166 us
  blocking collectives: 110 us -> 0 us
  matrix products: 28.6 us -> 0 us
  between operations: 18.4 us -> 0.64 us
  local copies, waits for them, and re-layouts: 21.6 us -> 6.64 us
    psum x4 -> x0, waiting for transfers between devices: 610 us -> none  [the longest x1 264 us: on_device(): lax.psum(jnp.einsum('ksm,kmr->sr', piece, kr_mic, preferred_element_type=...]
    pallas_call x0 -> x1, Pallas kernels: none -> 166 us  [on_device(): pl.pallas_call(kernel, out_shape=(jax.ShapeDtypeStruct((SRC_DEV, RANK), F...]
    another operation x27 -> x0, other arithmetic: 163 us -> none  [the longest x20 103 us: solve_rows(): lower = jnp.linalg.cholesky(system)]
    psum x1 -> x0, blocking collectives: 110 us -> none  [on_device(): time_mttkrp = lax.psum(time_term, ('mic', 'src'))]
    dot_general x8 -> x0, matrix products: 20.4 us -> none  [the longest x5 6.37 us: gram_of(): jnp.dot(factor.T, factor, precision=lax.Precision.HIGHEST, preferred_elem...]
    another operation x25 -> x0, local copies, waits for them, and re-layouts: 12.3 us -> none
  transfers between devices with their start and end apart: 4 -> 0, of which waited for: 4 -> 0; matrix products, arithmetic and copies ran while one was open for 6% -> 0% of each run, Pallas kernels for 0% -> 0%
where the time goes in v1:
time: 173 us
  Pallas kernels  166 us (96%)
  local copies, waits for them, and re-layouts  6.64 us (4%)
    pallas_call x1, Pallas kernels, on_device(): pl.pallas_call(kernel, out_shape=(jax.ShapeDtypeStruct((SRC_DEV, RANK), F...  166 us
    unnamed x10, local copies, waits for them, and re-layouts  6.64 us

profile of v1, /device:TPU:1, one launch (start us, length us, event | category | flops | bytes accessed | tf_op | source)
XLA Modules:
  0.0 173.1 jit_solution(6839081779895428464)
XLA Ops:
  0.6 0.7 copy.7.blk_ref
  1.4 0.0 copy-start
  1.4 2.2 %copy-done = bf16[32,512,128]{2,1,0:T(8,128)(2,1)S(1)} copy-done((bf16[32,512,128]{2,1,0:T(8,128)(2,1)S(1)}, bf16[32,512,128]{2,1,0:T(8,128)(2,1)}, u32[]{:S(2)}) %copy-start) | copy-done | bytes 4194328
  3.5 0.0 copy-start.1
  3.6 0.9 copy-done.1
  4.5 0.0 copy-start.2
  4.5 0.8 copy-done.2
  5.2 165.8 %shard_map.67 = (f32[512,256]{1,0:T(8,128)S(1)}, f32[128,256]{1,0:T(8,128)S(1)}, f32[32,256]{1,0:T(8,128)S(1)}) custom-call(bf16[32,512,128]{2,1,0:T(8,128)(2,1)S(1)} %copy-done, s32[8,1]{1,0:T(8,128)S(1)} %copy.7.blk_ref, f32[128,256]{1,0:T(8,128)S(1)} %copy-done.1, f32[32,256]{1,0:T(8,128)S(1)} %copy-done.2), custom_call_target="tpu_custom_call" | custom-call | tf_op jit(solution)/shard_map/pallas_call | solution.py:472
  171.0 0.8 copy.11
  171.8 0.7 copy.12
  172.5 0.6 copy.13
Async XLA Ops:
  1.4 2.2 %copy-start = (bf16[32,512,128]{2,1,0:T(8,128)(2,1)S(1)}, bf16[32,512,128]{2,1,0:T(8,128)(2,1)}, u32[]{:S(2)}) copy-start(bf16[32,512,128]{2,1,0:T(8,128)(2,1)} %x_hbm.1) | copy-start | bytes 12582916
  3.5 0.9 copy-start.1
  4.5 0.8 copy-start.2

commit v2 on v0

v2 whole, which is shorter than its diff:
```python
import functools

import jax
import jax.numpy as jnp
from jax import lax
from jax.experimental import pallas as pl
from jax.experimental.pallas import tpu as pltpu
from jax.sharding import PartitionSpec as P

MESH = pl.DeviceIdType.MESH
F32 = jnp.float32
BF16 = jnp.bfloat16

RANK = 256
SAMPLES = 32
SRC_DEV = 512
MIC_DEV = 128
SRC_BLK = 64
NX = 4
NZ = 16
NSRC = 8
NXS = NX * NSRC
SRC_ALL = SRC_DEV * NSRC
MIC_ALL = MIC_DEV * NX * NZ
BLK = 32
STAGES = 23


def exact_dot(a, b, dims=((1,), (0,))):
    return lax.dot_general(
        a, b, (dims, ((), ())), precision=lax.Precision.HIGHEST, preferred_element_type=F32
    )


def split3(a):
    first = a.astype(BF16)
    rest = a - first.astype(F32)
    second = rest.astype(BF16)
    third = (rest - second.astype(F32)).astype(BF16)
    return first, second, third


def outer_dot(a, b):
    a0, a1, a2 = split3(a)
    b0, b1, b2 = split3(b)
    left = jnp.concatenate([a0, a0, a1, a1, a0, a2], axis=0)
    right = jnp.concatenate([b0, b1, b0, b1, b2, b0], axis=0)
    return lax.dot_general(left, right, (((0,), (0,)), ((), ())), preferred_element_type=F32)


def twice(v):
    return jnp.concatenate([v, v], axis=1)


def eliminate(panel, rel, tile, first):
    sub = lax.broadcasted_iota(jnp.int32, (8, RANK), 0)
    sub_tile = lax.broadcasted_iota(jnp.int32, (8, 128), 0)
    groups = BLK // 8
    rows = [panel[8 * g : 8 * g + 8, :] for g in range(groups)]
    z_parts, w_parts = [], []
    for b in range(groups):
        lo = first + 8 * b
        col = {}
        for g in range(b, groups):
            part = rows[g][:, 128 * tile : 128 * tile + 128]
            col[g] = [jnp.broadcast_to(part[:, lo + j : lo + j + 1], (8, 128)) for j in range(8)]
        s = {}
        for k in range(8):
            for l in range(k, 8):
                s[k, l] = jnp.broadcast_to(col[b][l][k : k + 1, :], (8, 128))
        inside = (rel >= 8 * b) & (rel < 8 * b + 8)
        own = jnp.where(inside, jnp.where(rel == sub + 8 * b, -1.0, 0.0), rows[b])
        for g in range(b + 1, groups):
            rows[g] = jnp.where(inside, 0.0, rows[g])
        r = [jnp.broadcast_to(own[k : k + 1, :], (8, RANK)) for k in range(8)]
        inv = [None] * 8
        for j in range(0, 8, 2):
            a, m, d = s[j, j], s[j, j + 1], s[j + 1, j + 1]
            inv_det = 1.0 / (a * d - m * m)
            inv_a = 1.0 / a
            later = range(j + 2, 8)
            x = {l: s[j, l] for l in later}
            y = {l: s[j + 1, l] for l in later}
            u = {l: d * x[l] - m * y[l] for l in later}
            v = {l: a * y[l] - m * x[l] for l in later}
            for k in later:
                for l in range(k, 8):
                    s[k, l] = s[k, l] - (u[k] * x[l] + v[k] * y[l]) * inv_det
            f = m * inv_a
            r[j + 1] = r[j + 1] - twice(f) * r[j]
            inv[j] = inv_a
            inv[j + 1] = a * inv_det
            for k in later:
                r[k] = r[k] - twice(x[k] * inv_a) * r[j] - twice(v[k] * inv_det) * r[j + 1]
            for g in range(b + 1, groups):
                c1 = (col[g][j + 1] - col[g][j] * f) * inv[j + 1]
                c0 = col[g][j] * inv_a
                rows[g] = rows[g] - twice(c0) * r[j] - twice(c1) * r[j + 1]
                for l in later:
                    col[g][l] = col[g][l] - c0 * x[l] - c1 * (v[l] * inv_a)
        z, w = r[0], inv[0]
        for k in range(1, 8):
            z = jnp.where(sub == k, r[k], z)
            w = jnp.where(sub_tile == k, inv[k], w)
        z = jnp.where((rel >= 8 * b + 8) & (rel < BLK), 0.0, z)
        z_parts.append(z)
        w_parts.append(z * twice(w))
    return jnp.concatenate(z_parts, axis=0), jnp.concatenate(w_parts, axis=0)


def invert_block(a_ref, i):
    lane = lax.broadcasted_iota(jnp.int32, (8, RANK), 1)
    lane_row = lax.broadcasted_iota(jnp.int32, (1, RANK), 1)
    base = i * BLK
    rows = slice(base, base + BLK)
    z, w = eliminate(a_ref[rows, :], lane - base, base // 128, base % 128)
    inside = (lane_row >= base) & (lane_row < base + BLK)
    update = outer_dot(z, w)
    a_ref[rows, :] = jnp.zeros((BLK, RANK), F32)
    a_ref[...] = jnp.where(inside, 0.0, a_ref[...]) - update


def invert(a_ref, between=None):
    for i in range(RANK // BLK):
        invert_block(a_ref, i)
        if between is not None and i in between:
            between[i]()


def diagonal(gram):
    rows = lax.broadcasted_iota(jnp.int32, (RANK, RANK), 0)
    cols = lax.broadcasted_iota(jnp.int32, (RANK, RANK), 1)
    only = jnp.where(rows == cols, gram, 0.0)
    return jnp.sum(only, axis=0, keepdims=True), jnp.sum(only, axis=1, keepdims=True)


def scales_of(gram, count):
    row, col = diagonal(gram)
    return jnp.sqrt(row / count + 1e-06), jnp.sqrt(col / count + 1e-06)


def drain(ref, sem):
    pltpu.make_async_copy(ref, ref, sem).wait()


def ring_step(i):
    half = (i + 1) // 2
    return NZ // 2 + half - 2 * half * (i % 2)


def eight(k):
    return pl.ds(pl.multiple_of(k * 8, 8), 8)


def sweep(
    x_hbm,
    blk_hbm,
    mic_hbm,
    time_hbm,
    src_out,
    mic_out,
    time_out,
    blk_ref,
    mic_ref,
    time_ref,
    x_v,
    xt_v,
    kr_v,
    p_v,
    y_v,
    yx_v,
    y128_v,
    yz_v,
    yall_v,
    raw_v,
    low_v,
    gt_v,
    a_v,
    gn_v,
    g1_v,
    g1x_v,
    g1s_v,
    g1z_v,
    g1p_v,
    g1a_v,
    g2_v,
    g2s_v,
    g2p_v,
    g2a_v,
    mm_v,
    mr_v,
    mall_v,
    mraw_v,
    g3_v,
    g3x_v,
    g3s_v,
    g3z_v,
    g3p_v,
    g3a_v,
    t_v,
    ts_v,
    tp_v,
    tz_v,
    tq_v,
    ta_v,
    load_sem,
    send_sem,
    recv_sem,
):
    me_mic = lax.axis_index("mic")
    src = lax.axis_index("src")
    z = me_mic // NX
    x = me_mic % NX
    p = x * NSRC + src

    def at(zz, xx, ss):
        return (zz * NX + xx, ss)

    load_mic = pltpu.make_async_copy(mic_hbm, mic_ref, load_sem.at[0])
    load_time = pltpu.make_async_copy(time_hbm, time_ref, load_sem.at[1])
    load_blk = pltpu.make_async_copy(blk_hbm, blk_ref, load_sem.at[2])
    load = pltpu.make_async_copy(x_hbm, x_v, load_sem.at[3])
    load_mic.start()
    load_time.start()
    load_blk.start()
    load.start()

    barrier = pltpu.get_barrier_semaphore()

    def greet_z(d, c):
        pl.semaphore_signal(barrier, inc=1, device_id=at((z + d) % NZ, x, src), device_id_type=MESH)
        return c

    def greet_xs(d, c):
        q = (p + d) % NXS
        pl.semaphore_signal(
            barrier, inc=1, device_id=at(z, q // NSRC, q % NSRC), device_id_type=MESH
        )
        return c

    lax.fori_loop(1, NZ, greet_z, 0)
    lax.fori_loop(1, NXS, greet_xs, 0)

    waiting = {}

    def expect(stage, ref):
        waiting[stage] = [ref, True]

    def arrived(stage):
        drain(waiting[stage][0], recv_sem.at[stage])
        waiting[stage][1] = False

    def send(src_ref, dst_ref, stage, device):
        pltpu.make_async_remote_copy(
            src_ref=src_ref,
            dst_ref=dst_ref,
            send_sem=send_sem.at[stage],
            recv_sem=recv_sem.at[stage],
            device_id=device,
            device_id_type=MESH,
        ).start()

    def send_x(gram_ref, dst, stage):
        expect(stage, dst.at[pl.ds(0, NX - 1)])

        def one(d, c):
            xx = (x + d) % NX
            send(gram_ref.at[eight(xx * NSRC + src), :], dst.at[x], stage, at(z, xx, src))
            return c

        lax.fori_loop(1, NX, one, 0)
        dst[x] = gram_ref[eight(p), :]

    def send_z(piece_ref, dst, stage):
        expect(stage, dst.at[pl.ds(0, NZ - 1)])

        def one(i, c):
            send(piece_ref, dst.at[z], stage, at((z + ring_step(i)) % NZ, x, src))
            return c

        lax.fori_loop(0, NZ - 1, one, 0)
        dst[z] = piece_ref[...]

    def send_xs(piece_ref, dst, stage):
        expect(stage, dst.at[pl.ds(0, NXS - 1)])

        def one(d, c):
            q = (p + d) % NXS
            send(piece_ref, dst.at[p], stage, at(z, q // NSRC, q % NSRC))
            return c

        lax.fori_loop(1, NXS, one, 0)
        dst[p] = piece_ref[...]

    def send_src(piece_of, dst_ref, expected, stage):
        expect(stage, expected)

        def one(d, c):
            ss = (src + d) % NSRC
            send(piece_of(ss), dst_ref, stage, at(z, x, ss))
            return c

        lax.fori_loop(1, NSRC, one, 0)

    load_mic.wait()
    load_time.wait()
    mic = mic_ref[...]
    g1_v[...] = exact_dot(mic, mic, ((0,), (0,)))
    times = time_ref[...]
    gt_v[...] = exact_dot(times, times, ((0,), (0,)))
    mic_low = mic.astype(BF16).astype(F32)

    def make_kr(k, c):
        kr_v[pl.ds(pl.multiple_of(k * MIC_DEV, MIC_DEV), MIC_DEV), :] = (
            time_ref[pl.ds(k, 1), :] * mic_low
        ).astype(BF16)
        return c

    lax.fori_loop(0, SAMPLES, make_kr, 0)

    load_blk.wait()
    load.wait()
    for xx in range(NX):
        left = jnp.concatenate(
            [x_v[k, xx * 128 : (xx + 1) * 128, :] for k in range(SAMPLES)], axis=1
        )
        part = jnp.dot(left, kr_v[...], preferred_element_type=F32)
        for h in range(2):
            keep = blk_ref[0, xx * 2 + h].astype(F32)
            rows = slice(xx * 128 + h * 64, xx * 128 + (h + 1) * 64)
            y_v[rows, :] = part[h * 64 : (h + 1) * 64, :] * keep

    pl.semaphore_wait(barrier, NZ - 1 + NXS - 1)
    yield waiting

    send_x(g1_v, g1x_v, 0)

    for g in range(4):
        expect(3 + g, yx_v.at[0, pl.ds(0, 96), :])

        def row_group(dx, c, g=g):
            xx = (x + dx) % NX

            def one(i, c):
                zz = (z + ring_step(i)) % NZ
                send(
                    y_v.at[eight(xx * NZ + zz), :],
                    yx_v.at[dx - 1, eight(zz), :],
                    3 + g,
                    at(z, xx, src),
                )
                return c

            return lax.fori_loop(4 * g, 4 * g + 4, one, c)

        lax.fori_loop(1, NX, row_group, 0)

    arrived(0)
    g1s_v[...] = (g1x_v[0] + g1x_v[1]) + (g1x_v[2] + g1x_v[3])
    send_z(g1s_v, g1z_v, 1)

    expect(7, yz_v.at[pl.ds(0, NZ - 1)])
    for g in range(4):
        arrived(3 + g)

        def sum_send(i, c):
            zz = (z + ring_step(i)) % NZ
            rows = eight(zz)
            y128_v[rows, :] = (y_v[eight(x * NZ + zz), :] + yx_v[0, rows, :]) + (
                yx_v[1, rows, :] + yx_v[2, rows, :]
            )
            send(y128_v.at[rows, :], yz_v.at[i], 7, at(zz, x, src))
            return c

        lax.fori_loop(4 * g, min(4 * g + 4, NZ - 1), sum_send, 0)
    own = eight(z)
    yz_v[NZ - 1] = (y_v[eight(x * NZ + z), :] + yx_v[0, own, :]) + (
        yx_v[1, own, :] + yx_v[2, own, :]
    )
    yield waiting

    def flip(k, c):
        xt_v[k] = x_v[k].T
        return c

    lax.fori_loop(0, SAMPLES, flip, 0)

    arrived(7)
    mine = eight(x * NZ + z)
    yall_v[mine, :] = jnp.sum(yz_v[...], axis=0)
    for g in range(4):
        last = min(4 * g + 4, NZ - 1)
        expect(8 + g, yall_v.at[pl.ds(0, 8 * (last - 4 * g)), :])

        def back_z(i, c, g=g):
            zz = (z + ring_step(i)) % NZ
            send(yall_v.at[mine, :], yall_v.at[mine, :], 8 + g, at(zz, x, src))
            return c

        lax.fori_loop(4 * g, last, back_z, 0)

    expect(12, yall_v.at[pl.ds(0, 128 * (NX - 1)), :])

    def forward(rows):
        def one(dx, c):
            send(yall_v.at[rows, :], yall_v.at[rows, :], 12, at(z, (x + dx) % NX, src))
            return c

        lax.fori_loop(1, NX, one, 0)

    def forward_group(g):
        arrived(8 + g)

        def one(i, c):
            forward(eight(x * NZ + (z + NZ - ring_step(i)) % NZ))
            return c

        lax.fori_loop(4 * g, min(4 * g + 4, NZ - 1), one, 0)

    forward(mine)
    yield waiting

    arrived(1)
    g1p_v[...] = jnp.sum(g1z_v[...], axis=0)
    send_xs(g1p_v, g1a_v, 2)
    forward_group(3)
    forward_group(2)
    arrived(2)
    yield waiting
    a_v[...] = g1a_v[...].reshape(RANK, RANK) * gt_v[...] * (1.0 / (MIC_ALL * SAMPLES))
    invert(a_v, {1: lambda: forward_group(1), 3: lambda: forward_group(0)})
    yield waiting
    arrived(12)
    yield waiting
    raw = -exact_dot(yall_v[...], a_v[...])
    raw_v[...] = raw

    g2_v[...] = exact_dot(raw, raw, ((0,), (0,)))
    send_src(
        lambda ss: g2_v.at[eight(x * NSRC + ss), :],
        g2s_v.at[src],
        g2s_v.at[pl.ds(0, NSRC - 1)],
        13,
    )
    g2s_v[src] = g2_v[eight(p), :]

    for b in range(SRC_DEV // SRC_BLK):
        keep = blk_ref[0, b].astype(F32)
        rows = slice(b * SRC_BLK, (b + 1) * SRC_BLK)
        low_v[rows, :] = (raw_v[rows, :] * keep).astype(BF16)

    def mic_part(kk, acc):
        left = xt_v[pl.ds(kk * 8, 8)].reshape(8 * MIC_DEV, SRC_DEV)
        prod = jnp.dot(left, low_v[...], preferred_element_type=F32)
        for i in range(8):
            piece = prod[i * MIC_DEV : (i + 1) * MIC_DEV, :]
            p_v[kk * 8 + i] = piece
            acc = acc + time_ref[pl.ds(kk * 8 + i, 1), :] * piece
        return acc

    mm_v[...] = lax.fori_loop(0, SAMPLES // 8, mic_part, jnp.zeros((MIC_DEV, RANK), F32))

    def sixteen(k):
        return pl.ds(pl.multiple_of(k * 16, 16), 16)

    mic_rows = sixteen(src)
    send_src(
        lambda ss: mm_v.at[sixteen(ss), :], mr_v.at[src], mr_v.at[pl.ds(0, NSRC - 1)], 15
    )
    mr_v[src] = mm_v[mic_rows, :]
    yield waiting
    arrived(13)
    g2p_v[...] = jnp.sum(g2s_v[...], axis=0)
    send_xs(g2p_v, g2a_v, 14)
    arrived(15)
    mall_v[mic_rows, :] = jnp.sum(mr_v[...], axis=0)
    send_src(
        lambda ss: mall_v.at[mic_rows, :],
        mall_v.at[mic_rows, :],
        mall_v.at[pl.ds(0, 16 * (NSRC - 1)), :],
        16,
    )
    arrived(14)
    yield waiting
    gram_src = g2a_v[...].reshape(RANK, RANK)
    src_row, src_col = scales_of(gram_src, SRC_ALL)
    gram_src = gram_src / (src_row * src_col)
    gn_v[...] = gram_src
    a_v[...] = gram_src * gt_v[...] * (1.0 / (SRC_ALL * SAMPLES))
    invert(a_v)
    yield waiting
    arrived(16)
    mraw = -exact_dot(mall_v[...] / src_row, a_v[...])
    mraw_v[...] = mraw

    g3_v[...] = exact_dot(mraw, mraw, ((0,), (0,)))
    send_x(g3_v, g3x_v, 17)

    def time_part(kb, c):
        rows = [jnp.sum(p_v[kb * 8 + i] * mraw_v[...], axis=0, keepdims=True) for i in range(8)]
        piece = jnp.concatenate(rows, axis=0)
        t_v[kb] = piece[:, :128]
        t_v[kb + 4] = piece[:, 128:]
        return c

    lax.fori_loop(0, SAMPLES // 8, time_part, 0)
    send_src(lambda ss: t_v.at[ss], ts_v.at[src], ts_v.at[pl.ds(0, NSRC - 1)], 20)
    ts_v[src] = t_v[src]
    yield waiting

    arrived(17)
    g3s_v[...] = (g3x_v[0] + g3x_v[1]) + (g3x_v[2] + g3x_v[3])
    send_z(g3s_v, g3z_v, 18)
    arrived(20)
    tp_v[...] = jnp.sum(ts_v[...], axis=0)
    send_z(tp_v, tz_v, 21)
    src_out[...] = raw_v[...] / src_row
    arrived(18)
    yield waiting
    g3p_v[...] = jnp.sum(g3z_v[...], axis=0)
    send_xs(g3p_v, g3a_v, 19)
    arrived(21)
    tq_v[...] = jnp.sum(tz_v[...], axis=0)
    send_xs(tq_v, ta_v, 22)
    arrived(19)
    yield waiting

    gram_mic = g3a_v[...].reshape(RANK, RANK)
    mic_row, mic_col = scales_of(gram_mic, MIC_ALL)
    a_v[...] = gn_v[...] * (gram_mic / (mic_row * mic_col)) * (1.0 / (SRC_ALL * MIC_ALL))
    mic_out[...] = mraw_v[...] / mic_row
    invert(a_v)
    yield waiting

    arrived(22)
    parts = []
    for j in range(NSRC):
        parts.append((ta_v[j] + ta_v[8 + j]) + (ta_v[16 + j] + ta_v[24 + j]))
    total = jnp.concatenate(
        [jnp.concatenate([parts[kb], parts[kb + 4]], axis=1) for kb in range(4)], axis=0
    )
    total = total / (src_row * mic_row)
    time_raw = -exact_dot(total, a_v[...])
    time_diag = jnp.sum(time_raw * time_raw, axis=0, keepdims=True)
    time_out[...] = time_raw / jnp.sqrt(time_diag / SAMPLES + 1e-06)

    yield waiting


def kernel(*refs, stop=None):
    send_sem, recv_sem = refs[-2:]
    for count, waiting in enumerate(sweep(*refs)):
        if count == stop:
            break
    for stage, (ref, coming) in waiting.items():
        if coming:
            drain(ref, recv_sem.at[stage])
        drain(ref, send_sem.at[stage])


def on_device(tensor_slab, observed_blocks, mic_factor, time_factor, stop=None, collective_id=0, name=None):
    vmem = pl.BlockSpec(memory_space=pltpu.VMEM)
    return pl.pallas_call(
        functools.partial(kernel, stop=stop),
        name=name,
        out_shape=(
            jax.ShapeDtypeStruct((SRC_DEV, RANK), F32),
            jax.ShapeDtypeStruct((MIC_DEV, RANK), F32),
            jax.ShapeDtypeStruct((SAMPLES, RANK), F32),
        ),
        in_specs=[pl.BlockSpec(memory_space=pltpu.HBM)] * 4,
        out_specs=(vmem, vmem, vmem),
        scratch_shapes=[
            pltpu.SMEM((1, SRC_DEV // SRC_BLK), jnp.int32),
            pltpu.VMEM((MIC_DEV, RANK), F32),
            pltpu.VMEM((SAMPLES, RANK), F32),
            pltpu.VMEM((SAMPLES, SRC_DEV, MIC_DEV), BF16),
            pltpu.VMEM((SAMPLES, MIC_DEV, SRC_DEV), BF16),
            pltpu.VMEM((SAMPLES * MIC_DEV, RANK), BF16),
            pltpu.VMEM((SAMPLES, MIC_DEV, RANK), F32),
            pltpu.VMEM((SRC_DEV, RANK), F32),
            pltpu.VMEM((NX - 1, 128, RANK), F32),
            pltpu.VMEM((128, RANK), F32),
            pltpu.VMEM((NZ, 8, RANK), F32),
            pltpu.VMEM((SRC_DEV, RANK), F32),
            pltpu.VMEM((SRC_DEV, RANK), F32),
            pltpu.VMEM((SRC_DEV, RANK), BF16),
            pltpu.VMEM((RANK, RANK), F32),
            pltpu.VMEM((RANK, RANK), F32),
            pltpu.VMEM((RANK, RANK), F32),
            pltpu.VMEM((RANK, RANK), F32),
            pltpu.VMEM((NX, 8, RANK), F32),
            pltpu.VMEM((8, RANK), F32),
            pltpu.VMEM((NZ, 8, RANK), F32),
            pltpu.VMEM((8, RANK), F32),
            pltpu.VMEM((NXS, 8, RANK), F32),
            pltpu.VMEM((RANK, RANK), F32),
            pltpu.VMEM((NSRC, 8, RANK), F32),
            pltpu.VMEM((8, RANK), F32),
            pltpu.VMEM((NXS, 8, RANK), F32),
            pltpu.VMEM((MIC_DEV, RANK), F32),
            pltpu.VMEM((NSRC, 16, RANK), F32),
            pltpu.VMEM((MIC_DEV, RANK), F32),
            pltpu.VMEM((MIC_DEV, RANK), F32),
            pltpu.VMEM((RANK, RANK), F32),
            pltpu.VMEM((NX, 8, RANK), F32),
            pltpu.VMEM((8, RANK), F32),
            pltpu.VMEM((NZ, 8, RANK), F32),
            pltpu.VMEM((8, RANK), F32),
            pltpu.VMEM((NXS, 8, RANK), F32),
            pltpu.VMEM((NSRC, 8, 128), F32),
            pltpu.VMEM((NSRC, 8, 128), F32),
            pltpu.VMEM((8, 128), F32),
            pltpu.VMEM((NZ, 8, 128), F32),
            pltpu.VMEM((8, 128), F32),
            pltpu.VMEM((NXS, 8, 128), F32),
            pltpu.SemaphoreType.DMA((4,)),
            pltpu.SemaphoreType.DMA((STAGES,)),
            pltpu.SemaphoreType.DMA((STAGES,)),
        ],
        compiler_params=pltpu.CompilerParams(
            collective_id=collective_id, has_side_effects=True, vmem_limit_bytes=60 * 1024 * 1024
        ),
    )(tensor_slab, observed_blocks.reshape(1, SRC_DEV // SRC_BLK), mic_factor, time_factor)


def solution(mesh):
    placed = (P(None, "src", "mic"), P("src", "mic"), P("mic", None), P())
    return jax.shard_map(
        on_device,
        mesh=mesh,
        in_specs=placed,
        out_specs=(P("src", None), P("mic", None), P()),
        check_vma=False,
    )
```

time: 965 us -> 106 us (0.11)
  waiting for transfers between devices: 610 us -> 0 us
  other arithmetic: 167 us -> 0 us
  blocking collectives: 110 us -> 0 us
  Pallas kernels: 0 us -> 99.9 us
  matrix products: 28.6 us -> 0 us
  between operations: 18.4 us -> 0.64 us
  local copies, waits for them, and re-layouts: 21.6 us -> 4.81 us
    psum x4 -> x0, waiting for transfers between devices: 610 us -> none  [the longest x1 264 us: on_device(): lax.psum(jnp.einsum('ksm,kmr->sr', piece, kr_mic, preferred_element_type=...]
    another operation x27 -> x0, other arithmetic: 163 us -> none  [the longest x20 103 us: solve_rows(): lower = jnp.linalg.cholesky(system)]
    psum x1 -> x0, blocking collectives: 110 us -> none  [on_device(): time_mttkrp = lax.psum(time_term, ('mic', 'src'))]
    pallas_call x0 -> x1, Pallas kernels: none -> 99.9 us  [on_device(): pl.pallas_call(functools.partial(kernel, stop=stop), name=name, out_shape...]
    dot_general x8 -> x0, matrix products: 20.4 us -> none  [the longest x5 6.37 us: gram_of(): jnp.dot(factor.T, factor, precision=lax.Precision.HIGHEST, preferred_elem...]
    another operation x25 -> x0, local copies, waits for them, and re-layouts: 12.3 us -> none
  transfers between devices with their start and end apart: 4 -> 0, of which waited for: 4 -> 0; matrix products, arithmetic and copies ran while one was open for 6% -> 0% of each run, Pallas kernels for 0% -> 0%
where the time goes in v2:
time: 106 us; the launch traced here: 105 us
  Pallas kernels  99.9 us (94%)
  local copies, waits for them, and re-layouts  4.81 us (5%)
    pallas_call x1, Pallas kernels, on_device(): pl.pallas_call(functools.partial(kernel, stop=stop), name=name, out_shape...  99.9 us
    unnamed x3, local copies, waits for them, and re-layouts  4.81 us

profile of v2, /device:TPU:1, one launch (start us, length us, event | category | flops | bytes accessed | tf_op | source)
XLA Modules:
  0.0 105.4 jit_solution(1059494021332955457)
XLA Ops:
  0.6 99.9 %shard_map.67 = (f32[512,256]{1,0:T(8,128)}, f32[128,256]{1,0:T(8,128)}, f32[32,256]{1,0:T(8,128)}) custom-call(bf16[32,512,128]{2,1,0:T(8,128)(2,1)} %refs_0_.1, s32[1,8]{1,0:T(1,128)} %bitcast.1, f32[128,256]{1,0:T(8,128)} %refs_2_.1, f32[32,256]{1,0:T(8,128)} %refs_3_.1), custom_call_target="tpu_custom_call" | custom-call | tf_op jit(solution)/shard_map/pallas_call | solution.py:563
  100.6 1.9 %copy.10 = f32[512,256]{1,0:T(8,128)} copy(f32[512,256]{1,0:T(8,128)} %get-tuple-element.6) | data formatting | bytes 1048576
  102.4 1.6 %copy.11 = f32[128,256]{1,0:T(8,128)} copy(f32[128,256]{1,0:T(8,128)} %get-tuple-element.7) | data formatting | bytes 262144
  104.0 1.4 %copy.12 = f32[32,256]{1,0:T(8,128)} copy(f32[32,256]{1,0:T(8,128)} %get-tuple-element.8) | data formatting | bytes 65536

commit v3 on v2

--- a/solution.py
+++ b/solution.py
@@ -189,10 +189,10 @@
     g2a_v,
     mm_v,
     mr_v,
+    m16_v,
     mall_v,
     mraw_v,
     g3_v,
-    g3x_v,
     g3s_v,
     g3z_v,
     g3p_v,
@@ -203,6 +203,7 @@
     tz_v,
     tq_v,
     ta_v,
+    time_v,
     load_sem,
     send_sem,
     recv_sem,
@@ -379,11 +380,9 @@
     )
     yield waiting
 
-    def flip(k, c):
-        xt_v[k] = x_v[k].T
-        return c
-
-    lax.fori_loop(0, SAMPLES, flip, 0)
+    arrived(1)
+    g1p_v[...] = jnp.sum(g1z_v[...], axis=0)
+    send_xs(g1p_v, g1a_v, 2)
 
     arrived(7)
     mine = eight(x * NZ + z)
@@ -420,29 +419,39 @@
     forward(mine)
     yield waiting
 
-    arrived(1)
-    g1p_v[...] = jnp.sum(g1z_v[...], axis=0)
-    send_xs(g1p_v, g1a_v, 2)
-    forward_group(3)
-    forward_group(2)
+    def flip(k, c):
+        xt_v[k] = x_v[k].T
+        return c
+
+    lax.fori_loop(0, SAMPLES, flip, 0)
     arrived(2)
     yield waiting
     a_v[...] = g1a_v[...].reshape(RANK, RANK) * gt_v[...] * (1.0 / (MIC_ALL * SAMPLES))
-    invert(a_v, {1: lambda: forward_group(1), 3: lambda: forward_group(0)})
+    invert(
+        a_v,
+        {
+            0: lambda: forward_group(3),
+            2: lambda: forward_group(2),
+            4: lambda: forward_group(1),
+            6: lambda: forward_group(0),
+        },
+    )
     yield waiting
     arrived(12)
     yield waiting
     raw = -exact_dot(yall_v[...], a_v[...])
     raw_v[...] = raw
 
-    g2_v[...] = exact_dot(raw, raw, ((0,), (0,)))
+    half = x // 2
+    half_lanes = pl.ds(pl.multiple_of(half * 128, 128), 128)
+    g2_v[...] = exact_dot(raw_v[:, half_lanes], raw, ((0,), (0,)))
     send_src(
-        lambda ss: g2_v.at[eight(x * NSRC + ss), :],
+        lambda ss: g2_v.at[eight((x % 2) * NSRC + ss), :],
         g2s_v.at[src],
         g2s_v.at[pl.ds(0, NSRC - 1)],
         13,
     )
-    g2s_v[src] = g2_v[eight(p), :]
+    g2s_v[src] = g2_v[eight((x % 2) * NSRC + src), :]
 
     for b in range(SRC_DEV // SRC_BLK):
         keep = blk_ref[0, b].astype(F32)
@@ -473,13 +482,8 @@
     g2p_v[...] = jnp.sum(g2s_v[...], axis=0)
     send_xs(g2p_v, g2a_v, 14)
     arrived(15)
-    mall_v[mic_rows, :] = jnp.sum(mr_v[...], axis=0)
-    send_src(
-        lambda ss: mall_v.at[mic_rows, :],
-        mall_v.at[mic_rows, :],
-        mall_v.at[pl.ds(0, 16 * (NSRC - 1)), :],
-        16,
-    )
+    m16_v[...] = jnp.sum(mr_v[...], axis=0)
+    send_xs(m16_v, mall_v, 16)
     arrived(14)
     yield waiting
     gram_src = g2a_v[...].reshape(RANK, RANK)
@@ -490,31 +494,37 @@
     invert(a_v)
     yield waiting
     arrived(16)
-    mraw = -exact_dot(mall_v[...] / src_row, a_v[...])
+    mraw = -exact_dot(mall_v[...].reshape(NX * MIC_DEV, RANK) / src_row, a_v[...])
     mraw_v[...] = mraw
 
-    g3_v[...] = exact_dot(mraw, mraw, ((0,), (0,)))
-    send_x(g3_v, g3x_v, 17)
-
-    def time_part(kb, c):
-        rows = [jnp.sum(p_v[kb * 8 + i] * mraw_v[...], axis=0, keepdims=True) for i in range(8)]
-        piece = jnp.concatenate(rows, axis=0)
-        t_v[kb] = piece[:, :128]
-        t_v[kb + 4] = piece[:, 128:]
+    g3_v[...] = exact_dot(mraw_v[:, half_lanes], mraw, ((0,), (0,)))
+    g3s_v[...] = g3_v[eight((x % 2) * NSRC + src), :]
+    send_z(g3s_v, g3z_v, 18)
+
+    mic_own = pl.ds(pl.multiple_of(x * MIC_DEV, MIC_DEV), MIC_DEV)
+
+    def time_part(k, c):
+        t_v[k] = jnp.sum(p_v[k] * mraw_v[mic_own, :], axis=0, keepdims=True)
         return c
 
-    lax.fori_loop(0, SAMPLES // 8, time_part, 0)
-    send_src(lambda ss: t_v.at[ss], ts_v.at[src], ts_v.at[pl.ds(0, NSRC - 1)], 20)
-    ts_v[src] = t_v[src]
-    yield waiting
-
-    arrived(17)
-    g3s_v[...] = (g3x_v[0] + g3x_v[1]) + (g3x_v[2] + g3x_v[3])
-    send_z(g3s_v, g3z_v, 18)
+    lax.fori_loop(0, SAMPLES, time_part, 0)
+    expect(20, ts_v.at[pl.ds(0, NXS - 1)])
+
+    def send_sample(d, c):
+        q = (p + d) % NXS
+        send(t_v.at[q], ts_v.at[p], 20, at(z, q // NSRC, q % NSRC))
+        return c
+
+    lax.fori_loop(1, NXS, send_sample, 0)
+    ts_v[p] = t_v[p]
+    yield waiting
+
+    raw_v[...] = raw_v[...] / src_row
+    store_src = pltpu.make_async_copy(raw_v, src_out, load_sem.at[0])
+    store_src.start()
     arrived(20)
     tp_v[...] = jnp.sum(ts_v[...], axis=0)
     send_z(tp_v, tz_v, 21)
-    src_out[...] = raw_v[...] / src_row
     arrived(18)
     yield waiting
     g3p_v[...] = jnp.sum(g3z_v[...], axis=0)
@@ -528,21 +538,23 @@
     gram_mic = g3a_v[...].reshape(RANK, RANK)
     mic_row, mic_col = scales_of(gram_mic, MIC_ALL)
     a_v[...] = gn_v[...] * (gram_mic / (mic_row * mic_col)) * (1.0 / (SRC_ALL * MIC_ALL))
-    mic_out[...] = mraw_v[...] / mic_row
+    mraw_v[mic_own, :] = mraw_v[mic_own, :] / mic_row
+    store_mic = pltpu.make_async_copy(mraw_v.at[mic_own, :], mic_out, load_sem.at[1])
+    store_mic.start()
     invert(a_v)
     yield waiting
 
     arrived(22)
-    parts = []
-    for j in range(NSRC):
-        parts.append((ta_v[j] + ta_v[8 + j]) + (ta_v[16 + j] + ta_v[24 + j]))
-    total = jnp.concatenate(
-        [jnp.concatenate([parts[kb], parts[kb + 4]], axis=1) for kb in range(4)], axis=0
-    )
+    total = ta_v[...].reshape(SAMPLES, RANK)
     total = total / (src_row * mic_row)
     time_raw = -exact_dot(total, a_v[...])
     time_diag = jnp.sum(time_raw * time_raw, axis=0, keepdims=True)
-    time_out[...] = time_raw / jnp.sqrt(time_diag / SAMPLES + 1e-06)
+    time_v[...] = time_raw / jnp.sqrt(time_diag / SAMPLES + 1e-06)
+    store_time = pltpu.make_async_copy(time_v, time_out, load_sem.at[2])
+    store_time.start()
+    store_src.wait()
+    store_mic.wait()
+    store_time.wait()
 
     yield waiting
 
@@ -558,18 +570,27 @@
         drain(ref, send_sem.at[stage])
 
 
+def copy_out(*refs):
+    copies = [pltpu.make_async_copy(refs[i], refs[3 + i], refs[6].at[i]) for i in range(3)]
+    for copy in copies:
+        copy.start()
+    for copy in copies:
+        copy.wait()
+
+
 def on_device(tensor_slab, observed_blocks, mic_factor, time_factor, stop=None, collective_id=0, name=None):
-    vmem = pl.BlockSpec(memory_space=pltpu.VMEM)
-    return pl.pallas_call(
+    hbm = pl.BlockSpec(memory_space=pltpu.HBM)
+    outs = (
+        jax.ShapeDtypeStruct((SRC_DEV, RANK), F32),
+        jax.ShapeDtypeStruct((MIC_DEV, RANK), F32),
+        jax.ShapeDtypeStruct((SAMPLES, RANK), F32),
+    )
+    results = pl.pallas_call(
         functools.partial(kernel, stop=stop),
         name=name,
-        out_shape=(
-            jax.ShapeDtypeStruct((SRC_DEV, RANK), F32),
-            jax.ShapeDtypeStruct((MIC_DEV, RANK), F32),
-            jax.ShapeDtypeStruct((SAMPLES, RANK), F32),
-        ),
-        in_specs=[pl.BlockSpec(memory_space=pltpu.HBM)] * 4,
-        out_specs=(vmem, vmem, vmem),
+        out_shape=outs,
+        in_specs=[hbm] * 4,
+        out_specs=(hbm,) * 3,
         scratch_shapes=[
             pltpu.SMEM((1, SRC_DEV // SRC_BLK), jnp.int32),
             pltpu.VMEM((MIC_DEV, RANK), F32),
@@ -594,26 +615,27 @@
             pltpu.VMEM((NZ, 8, RANK), F32),
             pltpu.VMEM((8, RANK), F32),
             pltpu.VMEM((NXS, 8, RANK), F32),
-            pltpu.VMEM((RANK, RANK), F32),
+            pltpu.VMEM((128, RANK), F32),
             pltpu.VMEM((NSRC, 8, RANK), F32),
             pltpu.VMEM((8, RANK), F32),
             pltpu.VMEM((NXS, 8, RANK), F32),
             pltpu.VMEM((MIC_DEV, RANK), F32),
             pltpu.VMEM((NSRC, 16, RANK), F32),
-            pltpu.VMEM((MIC_DEV, RANK), F32),
-            pltpu.VMEM((MIC_DEV, RANK), F32),
-            pltpu.VMEM((RANK, RANK), F32),
-            pltpu.VMEM((NX, 8, RANK), F32),
+            pltpu.VMEM((16, RANK), F32),
+            pltpu.VMEM((NXS, 16, RANK), F32),
+            pltpu.VMEM((NX * MIC_DEV, RANK), F32),
+            pltpu.VMEM((128, RANK), F32),
             pltpu.VMEM((8, RANK), F32),
             pltpu.VMEM((NZ, 8, RANK), F32),
             pltpu.VMEM((8, RANK), F32),
             pltpu.VMEM((NXS, 8, RANK), F32),
-            pltpu.VMEM((NSRC, 8, 128), F32),
-            pltpu.VMEM((NSRC, 8, 128), F32),
-            pltpu.VMEM((8, 128), F32),
-            pltpu.VMEM((NZ, 8, 128), F32),
-            pltpu.VMEM((8, 128), F32),
-            pltpu.VMEM((NXS, 8, 128), F32),
+            pltpu.VMEM((NXS, 1, RANK), F32),
+            pltpu.VMEM((NXS, 1, RANK), F32),
+            pltpu.VMEM((1, RANK), F32),
+            pltpu.VMEM((NZ, 1, RANK), F32),
+            pltpu.VMEM((1, RANK), F32),
+            pltpu.VMEM((NXS, 1, RANK), F32),
+            pltpu.VMEM((SAMPLES, RANK), F32),
             pltpu.SemaphoreType.DMA((4,)),
             pltpu.SemaphoreType.DMA((STAGES,)),
             pltpu.SemaphoreType.DMA((STAGES,)),
@@ -622,6 +644,14 @@
             collective_id=collective_id, has_side_effects=True, vmem_limit_bytes=60 * 1024 * 1024
         ),
     )(tensor_slab, observed_blocks.reshape(1, SRC_DEV // SRC_BLK), mic_factor, time_factor)
+    return pl.pallas_call(
+        copy_out,
+        out_shape=outs,
+        in_specs=[hbm] * 3,
+        out_specs=(hbm,) * 3,
+        scratch_shapes=[pltpu.SemaphoreType.DMA((3,))],
+        compiler_params=pltpu.CompilerParams(vmem_limit_bytes=60 * 1024 * 1024),
+    )(*results)
 
 
 def solution(mesh):

time: 106 us -> 121 us (1.14)
  Pallas kernels: 99.9 us -> 120 us
  local copies, waits for them, and re-layouts: 4.81 us -> 0 us
    pallas_call x0 -> x1, Pallas kernels: none -> 22 us  [on_device(): pl.pallas_call(copy_out, out_shape=outs, in_specs=[hbm] * 3, out_specs=(h...]
    unnamed x3 -> x0, local copies, waits for them, and re-layouts: 4.81 us -> none
    pallas_call x1, Pallas kernels: 99.9 us -> 97.9 us  [on_device(): pl.pallas_call(functools.partial(kernel, stop=stop), name=name, out_shape...]
where the time goes in v3:
time: 121 us
  Pallas kernels  120 us (99%)
    pallas_call x1, Pallas kernels, on_device(): pl.pallas_call(functools.partial(kernel, stop=stop), name=name, out_shape...  97.9 us
    pallas_call x1, Pallas kernels, on_device(): pl.pallas_call(copy_out, out_shape=outs, in_specs=[hbm] * 3, out_specs=(h...  22 us

profile of v3, /device:TPU:1, one launch (start us, length us, event | category | flops | bytes accessed | tf_op | source)
XLA Modules:
  0.0 120.6 jit_solution(12214527822031426322)
XLA Ops:
  0.6 97.9 %shard_map.67 = (f32[512,256]{1,0:T(8,128)}, f32[128,256]{1,0:T(8,128)}, f32[32,256]{1,0:T(8,128)}) custom-call(bf16[32,512,128]{2,1,0:T(8,128)(2,1)} %refs_0_.1, s32[1,8]{1,0:T(1,128)} %bitcast.1, f32[128,256]{1,0:T(8,128)} %refs_2_.1, f32[32,256]{1,0:T(8,128)} %refs_3_.1), custom_call_target="tpu_custom_call" | custom-call | tf_op jit(solution)/shard_map/pallas_call | solution.py:588
  98.5 22.0 %shard_map.68 = (f32[512,256]{1,0:T(8,128)}, f32[128,256]{1,0:T(8,128)}, f32[32,256]{1,0:T(8,128)}) custom-call(f32[512,256]{1,0:T(8,128)} %get-tuple-element.6.refs_0_, f32[128,256]{1,0:T(8,128)} %get-tuple-element.7.refs_1_, f32[32,256]{1,0:T(8,128)} %get-tuple-element.8.refs_2_), custom_call_target="tpu_custom_call" | custom-call | tf_op jit(solution)/shard_map/pallas_call | solution.py:647

commit v4 on v3

--- a/solution.py
+++ b/solution.py
@@ -143,9 +143,9 @@
     pltpu.make_async_copy(ref, ref, sem).wait()
 
 
-def ring_step(i):
+def ring_step(i, size=NZ):
     half = (i + 1) // 2
-    return NZ // 2 + half - 2 * half * (i % 2)
+    return size // 2 + half - 2 * half * (i % 2)
 
 
 def eight(k):
@@ -228,8 +228,9 @@
 
     barrier = pltpu.get_barrier_semaphore()
 
-    def greet_z(d, c):
-        pl.semaphore_signal(barrier, inc=1, device_id=at((z + d) % NZ, x, src), device_id_type=MESH)
+    def greet_z(i, c):
+        zz = (z + ring_step(i)) % NZ
+        pl.semaphore_signal(barrier, inc=1, device_id=at(zz, x, src), device_id_type=MESH)
         return c
 
     def greet_xs(d, c):
@@ -239,7 +240,7 @@
         )
         return c
 
-    lax.fori_loop(1, NZ, greet_z, 0)
+    lax.fori_loop(0, NZ - 1, greet_z, 0)
     lax.fori_loop(1, NXS, greet_xs, 0)
 
     waiting = {}
@@ -282,26 +283,31 @@
         lax.fori_loop(0, NZ - 1, one, 0)
         dst[z] = piece_ref[...]
 
+    def plane_step(i):
+        xx = (x + ring_step(i // NSRC, NX)) % NX
+        yy = (src // 2 + ring_step(i // 2 % (NSRC // 2), NSRC // 2)) % (NSRC // 2)
+        return xx, yy * 2 + (src % 2 + 1 + i) % 2
+
     def send_xs(piece_ref, dst, stage):
         expect(stage, dst.at[pl.ds(0, NXS - 1)])
 
-        def one(d, c):
-            q = (p + d) % NXS
-            send(piece_ref, dst.at[p], stage, at(z, q // NSRC, q % NSRC))
-            return c
-
-        lax.fori_loop(1, NXS, one, 0)
+        def one(i, c):
+            xx, ss = plane_step(i)
+            send(piece_ref, dst.at[p], stage, at(z, xx, ss))
+            return c
+
+        lax.fori_loop(0, NXS - 1, one, 0)
         dst[p] = piece_ref[...]
 
     def send_src(piece_of, dst_ref, expected, stage):
         expect(stage, expected)
 
-        def one(d, c):
-            ss = (src + d) % NSRC
+        def one(i, c):
+            ss = plane_step(NXS - NSRC + i)[1]
             send(piece_of(ss), dst_ref, stage, at(z, x, ss))
             return c
 
-        lax.fori_loop(1, NSRC, one, 0)
+        lax.fori_loop(0, NSRC - 1, one, 0)
 
     load_mic.wait()
     load_time.wait()
@@ -339,7 +345,8 @@
     for g in range(4):
         expect(3 + g, yx_v.at[0, pl.ds(0, 96), :])
 
-        def row_group(dx, c, g=g):
+        def row_group(ix, c, g=g):
+            dx = ring_step(ix, NX)
             xx = (x + dx) % NX
 
             def one(i, c):
@@ -354,7 +361,7 @@
 
             return lax.fori_loop(4 * g, 4 * g + 4, one, c)
 
-        lax.fori_loop(1, NX, row_group, 0)
+        lax.fori_loop(0, NX - 1, row_group, 0)
 
     arrived(0)
     g1s_v[...] = (g1x_v[0] + g1x_v[1]) + (g1x_v[2] + g1x_v[3])
@@ -380,6 +387,12 @@
     )
     yield waiting
 
+    def flip(k, c):
+        xt_v[k] = x_v[k].T
+        return c
+
+    lax.fori_loop(0, SAMPLES, flip, 0)
+
     arrived(1)
     g1p_v[...] = jnp.sum(g1z_v[...], axis=0)
     send_xs(g1p_v, g1a_v, 2)
@@ -401,11 +414,12 @@
     expect(12, yall_v.at[pl.ds(0, 128 * (NX - 1)), :])
 
     def forward(rows):
-        def one(dx, c):
-            send(yall_v.at[rows, :], yall_v.at[rows, :], 12, at(z, (x + dx) % NX, src))
-            return c
-
-        lax.fori_loop(1, NX, one, 0)
+        def one(ix, c):
+            xx = (x + ring_step(ix, NX)) % NX
+            send(yall_v.at[rows, :], yall_v.at[rows, :], 12, at(z, xx, src))
+            return c
+
+        lax.fori_loop(0, NX - 1, one, 0)
 
     def forward_group(g):
         arrived(8 + g)
@@ -419,23 +433,12 @@
     forward(mine)
     yield waiting
 
-    def flip(k, c):
-        xt_v[k] = x_v[k].T
-        return c
-
-    lax.fori_loop(0, SAMPLES, flip, 0)
+    forward_group(3)
+    forward_group(2)
     arrived(2)
     yield waiting
     a_v[...] = g1a_v[...].reshape(RANK, RANK) * gt_v[...] * (1.0 / (MIC_ALL * SAMPLES))
-    invert(
-        a_v,
-        {
-            0: lambda: forward_group(3),
-            2: lambda: forward_group(2),
-            4: lambda: forward_group(1),
-            6: lambda: forward_group(0),
-        },
-    )
+    invert(a_v, {1: lambda: forward_group(1), 3: lambda: forward_group(0)})
     yield waiting
     arrived(12)
     yield waiting
@@ -510,12 +513,12 @@
     lax.fori_loop(0, SAMPLES, time_part, 0)
     expect(20, ts_v.at[pl.ds(0, NXS - 1)])
 
-    def send_sample(d, c):
-        q = (p + d) % NXS
-        send(t_v.at[q], ts_v.at[p], 20, at(z, q // NSRC, q % NSRC))
+    def send_sample(i, c):
+        xx, ss = plane_step(i)
+        send(t_v.at[xx * NSRC + ss], ts_v.at[p], 20, at(z, xx, ss))
         return c
 
-    lax.fori_loop(1, NXS, send_sample, 0)
+    lax.fori_loop(0, NXS - 1, send_sample, 0)
     ts_v[p] = t_v[p]
     yield waiting
 
@@ -570,12 +573,10 @@
         drain(ref, send_sem.at[stage])
 
 
-def copy_out(*refs):
-    copies = [pltpu.make_async_copy(refs[i], refs[3 + i], refs[6].at[i]) for i in range(3)]
-    for copy in copies:
-        copy.start()
-    for copy in copies:
-        copy.wait()
+def copy_out(src_in, mic_in, time_in, src_out, mic_out, time_out):
+    src_out[...] = src_in[...]
+    mic_out[...] = mic_in[...]
+    time_out[...] = time_in[...]
 
 
 def on_device(tensor_slab, observed_blocks, mic_factor, time_factor, stop=None, collective_id=0, name=None):
@@ -644,12 +645,12 @@
             collective_id=collective_id, has_side_effects=True, vmem_limit_bytes=60 * 1024 * 1024
         ),
     )(tensor_slab, observed_blocks.reshape(1, SRC_DEV // SRC_BLK), mic_factor, time_factor)
+    vmem = pl.BlockSpec(memory_space=pltpu.VMEM)
     return pl.pallas_call(
         copy_out,
         out_shape=outs,
-        in_specs=[hbm] * 3,
-        out_specs=(hbm,) * 3,
-        scratch_shapes=[pltpu.SemaphoreType.DMA((3,))],
+        in_specs=[vmem] * 3,
+        out_specs=(vmem,) * 3,
         compiler_params=pltpu.CompilerParams(vmem_limit_bytes=60 * 1024 * 1024),
     )(*results)
 

time: 121 us -> 99.5 us (0.82)
  Pallas kernels: 120 us -> 98.7 us
    pallas_call x1, Pallas kernels: 22 us -> 1.97 us  [on_device(): pl.pallas_call(copy_out, out_shape=outs, in_specs=[vmem] * 3, out_specs=(...]
where the time goes in v4:
time: 99.5 us; the launch traced here: 99.4 us
  Pallas kernels  98.7 us (99%)
    pallas_call x1, Pallas kernels, on_device(): pl.pallas_call(functools.partial(kernel, stop=stop), name=name, out_shape...  96.7 us

profile of v4, /device:TPU:1, one launch (start us, length us, event | category | flops | bytes accessed | tf_op | source)
XLA Modules:
  0.0 99.4 jit_solution(4394326528889672449)
XLA Ops:
  0.6 96.7 %shard_map.67 = (f32[512,256]{1,0:T(8,128)}, f32[128,256]{1,0:T(8,128)}, f32[32,256]{1,0:T(8,128)}) custom-call(bf16[32,512,128]{2,1,0:T(8,128)(2,1)} %refs_0_.1, s32[1,8]{1,0:T(1,128)} %bitcast.1, f32[128,256]{1,0:T(8,128)} %refs_2_.1, f32[32,256]{1,0:T(8,128)} %refs_3_.1), custom_call_target="tpu_custom_call" | custom-call | tf_op jit(solution)/shard_map/pallas_call | solution.py:589
  97.4 2.0 %shard_map.68 = (f32[512,256]{1,0:T(8,128)}, f32[128,256]{1,0:T(8,128)}, f32[32,256]{1,0:T(8,128)}) custom-call(f32[512,256]{1,0:T(8,128)} %get-tuple-element.6.src_in, f32[128,256]{1,0:T(8,128)} %get-tuple-element.7.mic_in, f32[32,256]{1,0:T(8,128)} %get-tuple-element.8.time_in), custom_call_target="tpu_custom_call" | custom-call | tf_op jit(solution)/shard_map/pallas_call | solution.py:649

commit v5 on v4

--- a/solution.py
+++ b/solution.py
@@ -23,7 +23,7 @@
 SRC_ALL = SRC_DEV * NSRC
 MIC_ALL = MIC_DEV * NX * NZ
 BLK = 32
-STAGES = 23
+STAGES = 27
 
 
 def exact_dot(a, b, dims=((1,), (0,))):
@@ -180,9 +180,14 @@
     g1_v,
     g1x_v,
     g1s_v,
-    g1z_v,
-    g1p_v,
-    g1a_v,
+    c1_v,
+    d1_v,
+    c1z_v,
+    d1z_v,
+    c1s_v,
+    d1s_v,
+    c1a_v,
+    d1a_v,
     g2_v,
     g2s_v,
     g2p_v,
@@ -194,9 +199,14 @@
     mraw_v,
     g3_v,
     g3s_v,
-    g3z_v,
-    g3p_v,
-    g3a_v,
+    c3_v,
+    d3_v,
+    c3z_v,
+    d3z_v,
+    c3s_v,
+    d3s_v,
+    c3a_v,
+    d3a_v,
     t_v,
     ts_v,
     tp_v,
@@ -213,6 +223,8 @@
     z = me_mic // NX
     x = me_mic % NX
     p = x * NSRC + src
+    core = src % 2
+    q = p // 2
 
     def at(zz, xx, ss):
         return (zz * NX + xx, ss)
@@ -246,11 +258,22 @@
     waiting = {}
 
     def expect(stage, ref):
-        waiting[stage] = [ref, True]
+        waiting[stage] = [lambda sem: drain(ref, sem), lambda sem: drain(ref, sem), True]
+
+    def expect_by_core(stage, received, sent):
+        def by_core(refs):
+            def wait(sem):
+                for which in range(2):
+                    if refs[which] is not None:
+                        pl.when(core == which)(functools.partial(drain, refs[which], sem))
+
+            return wait
+
+        waiting[stage] = [by_core(received), by_core(sent), True]
 
     def arrived(stage):
-        drain(waiting[stage][0], recv_sem.at[stage])
-        waiting[stage][1] = False
+        waiting[stage][0](recv_sem.at[stage])
+        waiting[stage][2] = False
 
     def send(src_ref, dst_ref, stage, device):
         pltpu.make_async_remote_copy(
@@ -265,13 +288,14 @@
     def send_x(gram_ref, dst, stage):
         expect(stage, dst.at[pl.ds(0, NX - 1)])
 
-        def one(d, c):
-            xx = (x + d) % NX
-            send(gram_ref.at[eight(xx * NSRC + src), :], dst.at[x], stage, at(z, xx, src))
+        def one(i, c):
+            xx = (x + ring_step(i, NX)) % NX
+            rows = eight(core * 16 + (xx * NSRC + src) // 2)
+            send(gram_ref.at[rows, :], dst.at[x], stage, at(z, xx, src))
             return c
 
-        lax.fori_loop(1, NX, one, 0)
-        dst[x] = gram_ref[eight(p), :]
+        lax.fori_loop(0, NX - 1, one, 0)
+        dst[x] = gram_ref[eight(core * 16 + q), :]
 
     def send_z(piece_ref, dst, stage):
         expect(stage, dst.at[pl.ds(0, NZ - 1)])
@@ -298,6 +322,61 @@
 
         lax.fori_loop(0, NXS - 1, one, 0)
         dst[p] = piece_ref[...]
+
+    core_lanes = pl.ds(pl.multiple_of(core * 128, 128), 128)
+
+    def corner_z(piece_ref, one_v, two_v, one_z, two_z, stage):
+        one_v[...] = piece_ref[:, core_lanes]
+        send_z(one_v, one_z, stage)
+        half = two_z.at[pl.ds(0, NZ - 1)]
+
+        @pl.when(core == 0)
+        def _():
+            two_v[...] = piece_ref[:, 128:]
+            send_z(two_v, two_z, stage + 1)
+
+        expect_by_core(stage + 1, (half, None), (half, None))
+
+    def corner_sum(one_v, two_v, one_z, two_z, stage):
+        arrived(stage)
+        one_v[...] = jnp.sum(one_z[...], axis=0)
+        arrived(stage + 1)
+
+        @pl.when(core == 0)
+        def _():
+            two_v[...] = jnp.sum(two_z[...], axis=0)
+
+    def corner_xs(one_v, two_v, one_a, two_a, stage):
+        send_xs(one_v, one_a, stage)
+
+        @pl.when(core == 0)
+        def _():
+            def one(i, c):
+                xx, ss = plane_step(i)
+                send(two_v, two_a.at[q], stage + 1, at(z, xx, ss))
+                return c
+
+            lax.fori_loop(0, NXS - 1, one, 0)
+            two_a[q] = two_v[...]
+
+        expect_by_core(
+            stage + 1,
+            (two_a.at[pl.ds(0, NXS // 2 - 1)], two_a),
+            (one_a.at[pl.ds(0, NXS - 1)], None),
+        )
+
+    def corner_gram(one_a, two_a, stage):
+        arrived(stage)
+        arrived(stage + 1)
+        ones = one_a[...].reshape(NXS // 2, 2, 8, 128)
+        upper = two_a[...].reshape(128, 128)
+        return jnp.concatenate(
+            [
+                jnp.concatenate([ones[:, 0].reshape(128, 128), upper], axis=1),
+                jnp.concatenate([upper.T, ones[:, 1].reshape(128, 128)], axis=1),
+            ],
+            axis=0,
+        )
 
     def send_src(piece_of, dst_ref, expected, stage):
         expect(stage, expected)
@@ -365,7 +444,7 @@
 
     arrived(0)
     g1s_v[...] = (g1x_v[0] + g1x_v[1]) + (g1x_v[2] + g1x_v[3])
-    send_z(g1s_v, g1z_v, 1)
+    corner_z(g1s_v, c1_v, d1_v, c1z_v, d1z_v, 23)
 
     expect(7, yz_v.at[pl.ds(0, NZ - 1)])
     for g in range(4):
@@ -393,9 +472,8 @@
 
     lax.fori_loop(0, SAMPLES, flip, 0)
 
-    arrived(1)
-    g1p_v[...] = jnp.sum(g1z_v[...], axis=0)
-    send_xs(g1p_v, g1a_v, 2)
+    corner_sum(c1s_v, d1s_v, c1z_v, d1z_v, 23)
+    corner_xs(c1s_v, d1s_v, c1a_v, d1a_v, 1)
 
     arrived(7)
     mine = eight(x * NZ + z)
@@ -435,9 +513,9 @@
 
     forward_group(3)
     forward_group(2)
-    arrived(2)
-    yield waiting
-    a_v[...] = g1a_v[...].reshape(RANK, RANK) * gt_v[...] * (1.0 / (MIC_ALL * SAMPLES))
+    gram_mic = corner_gram(c1a_v, d1a_v, 1)
+    yield waiting
+    a_v[...] = gram_mic * gt_v[...] * (1.0 / (MIC_ALL * SAMPLES))
     invert(a_v, {1: lambda: forward_group(1), 3: lambda: forward_group(0)})
     yield waiting
     arrived(12)
@@ -500,9 +578,9 @@
     mraw = -exact_dot(mall_v[...].reshape(NX * MIC_DEV, RANK) / src_row, a_v[...])
     mraw_v[...] = mraw
 
-    g3_v[...] = exact_dot(mraw_v[:, half_lanes], mraw, ((0,), (0,)))
-    g3s_v[...] = g3_v[eight((x % 2) * NSRC + src), :]
-    send_z(g3s_v, g3z_v, 18)
+    g3_v[...] = exact_dot(mraw_v[:, core_lanes], mraw, ((0,), (0,)))
+    g3s_v[...] = g3_v[eight(q), :]
+    corner_z(g3s_v, c3_v, d3_v, c3z_v, d3z_v, 25)
 
     mic_own = pl.ds(pl.multiple_of(x * MIC_DEV, MIC_DEV), MIC_DEV)
 
@@ -528,17 +606,15 @@
     arrived(20)
     tp_v[...] = jnp.sum(ts_v[...], axis=0)
     send_z(tp_v, tz_v, 21)
-    arrived(18)
-    yield waiting
-    g3p_v[...] = jnp.sum(g3z_v[...], axis=0)
-    send_xs(g3p_v, g3a_v, 19)
+    corner_sum(c3s_v, d3s_v, c3z_v, d3z_v, 25)
+    yield waiting
+    corner_xs(c3s_v, d3s_v, c3a_v, d3a_v, 18)
     arrived(21)
     tq_v[...] = jnp.sum(tz_v[...], axis=0)
     send_xs(tq_v, ta_v, 22)
-    arrived(19)
-    yield waiting
-
-    gram_mic = g3a_v[...].reshape(RANK, RANK)
+    gram_mic = corner_gram(c3a_v, d3a_v, 18)
+    yield waiting
+
     mic_row, mic_col = scales_of(gram_mic, MIC_ALL)
     a_v[...] = gn_v[...] * (gram_mic / (mic_row * mic_col)) * (1.0 / (SRC_ALL * MIC_ALL))
     mraw_v[mic_own, :] = mraw_v[mic_own, :] / mic_row
@@ -567,10 +643,10 @@
     for count, waiting in enumerate(sweep(*refs)):
         if count == stop:
             break
-    for stage, (ref, coming) in waiting.items():
+    for stage, (receive, leave, coming) in waiting.items():
         if coming:
-            drain(ref, recv_sem.at[stage])
-        drain(ref, send_sem.at[stage])
+            receive(recv_sem.at[stage])
+        leave(send_sem.at[stage])
 
 
 def copy_out(src_in, mic_in, time_in, src_out, mic_out, time_out):
@@ -613,9 +689,14 @@
             pltpu.VMEM((RANK, RANK), F32),
             pltpu.VMEM((NX, 8, RANK), F32),
             pltpu.VMEM((8, RANK), F32),
-            pltpu.VMEM((NZ, 8, RANK), F32),
-            pltpu.VMEM((8, RANK), F32),
-            pltpu.VMEM((NXS, 8, RANK), F32),
+            pltpu.VMEM((8, 128), F32),
+            pltpu.VMEM((8, 128), F32),
+            pltpu.VMEM((NZ, 8, 128), F32),
+            pltpu.VMEM((NZ, 8, 128), F32),
+            pltpu.VMEM((8, 128), F32),
+            pltpu.VMEM((8, 128), F32),
+            pltpu.VMEM((NXS, 8, 128), F32),
+            pltpu.VMEM((NXS // 2, 8, 128), F32),
             pltpu.VMEM((128, RANK), F32),
             pltpu.VMEM((NSRC, 8, RANK), F32),
             pltpu.VMEM((8, RANK), F32),
@@ -627,9 +708,14 @@
             pltpu.VMEM((NX * MIC_DEV, RANK), F32),
             pltpu.VMEM((128, RANK), F32),
             pltpu.VMEM((8, RANK), F32),
-            pltpu.VMEM((NZ, 8, RANK), F32),
-            pltpu.VMEM((8, RANK), F32),
-            pltpu.VMEM((NXS, 8, RANK), F32),
+            pltpu.VMEM((8, 128), F32),
+            pltpu.VMEM((8, 128), F32),
+            pltpu.VMEM((NZ, 8, 128), F32),
+            pltpu.VMEM((NZ, 8, 128), F32),
+            pltpu.VMEM((8, 128), F32),
+            pltpu.VMEM((8, 128), F32),
+            pltpu.VMEM((NXS, 8, 128), F32),
+            pltpu.VMEM((NXS // 2, 8, 128), F32),
             pltpu.VMEM((NXS, 1, RANK), F32),
             pltpu.VMEM((NXS, 1, RANK), F32),
             pltpu.VMEM((1, RANK), F32),

time: 99.5 us -> 99.6 us (level)
  no operation moved by 1% of the time
where the time goes in v5:
time: 99.6 us; the launch traced here: 99.4 us
  Pallas kernels  98.8 us (99%)
    pallas_call x1, Pallas kernels, on_device(): pl.pallas_call(functools.partial(kernel, stop=stop), name=name, out_shape...  96.8 us

profile of v5, /device:TPU:1, one launch (start us, length us, event | category | flops | bytes accessed | tf_op | source)
XLA Modules:
  0.0 99.4 jit_solution(1878758316037792783)
XLA Ops:
  0.6 96.8 %shard_map.67 = (f32[512,256]{1,0:T(8,128)}, f32[128,256]{1,0:T(8,128)}, f32[32,256]{1,0:T(8,128)}) custom-call(bf16[32,512,128]{2,1,0:T(8,128)(2,1)} %refs_0_.1, s32[1,8]{1,0:T(1,128)} %bitcast.1, f32[128,256]{1,0:T(8,128)} %refs_2_.1, f32[32,256]{1,0:T(8,128)} %refs_3_.1), custom_call_target="tpu_custom_call" | custom-call | tf_op jit(solution)/shard_map/pallas_call | solution.py:665
  97.5 2.0 %shard_map.68 = (f32[512,256]{1,0:T(8,128)}, f32[128,256]{1,0:T(8,128)}, f32[32,256]{1,0:T(8,128)}) custom-call(f32[512,256]{1,0:T(8,128)} %get-tuple-element.6.src_in, f32[128,256]{1,0:T(8,128)} %get-tuple-element.7.mic_in, f32[32,256]{1,0:T(8,128)} %get-tuple-element.8.time_in), custom_call_target="tpu_custom_call" | custom-call | tf_op jit(solution)/shard_map/pallas_call | solution.py:735

commit v6 on v5

--- a/solution.py
+++ b/solution.py
@@ -52,7 +52,7 @@
     return jnp.concatenate([v, v], axis=1)
 
 
-def eliminate(panel, rel, tile, first):
+def eliminate(panel, rel, tile, first, unit):
     sub = lax.broadcasted_iota(jnp.int32, (8, RANK), 0)
     sub_tile = lax.broadcasted_iota(jnp.int32, (8, 128), 0)
     groups = BLK // 8
@@ -69,7 +69,7 @@
             for l in range(k, 8):
                 s[k, l] = jnp.broadcast_to(col[b][l][k : k + 1, :], (8, 128))
         inside = (rel >= 8 * b) & (rel < 8 * b + 8)
-        own = jnp.where(inside, jnp.where(rel == sub + 8 * b, -1.0, 0.0), rows[b])
+        own = jnp.where(inside, jnp.where(rel == sub + 8 * b, unit, 0.0), rows[b])
         for g in range(b + 1, groups):
             rows[g] = jnp.where(inside, 0.0, rows[g])
         r = [jnp.broadcast_to(own[k : k + 1, :], (8, RANK)) for k in range(8)]
@@ -113,7 +113,7 @@
     lane_row = lax.broadcasted_iota(jnp.int32, (1, RANK), 1)
     base = i * BLK
     rows = slice(base, base + BLK)
-    z, w = eliminate(a_ref[rows, :], lane - base, base // 128, base % 128)
+    z, w = eliminate(a_ref[rows, :], lane - base, base // 128, base % 128, -1.0)
     inside = (lane_row >= base) & (lane_row < base + BLK)
     update = outer_dot(z, w)
     a_ref[rows, :] = jnp.zeros((BLK, RANK), F32)
@@ -125,6 +125,23 @@
         invert_block(a_ref, i)
         if between is not None and i in between:
             between[i]()
+
+
+def factor(a_ref, z_ref, w_ref):
+    lane = lax.broadcasted_iota(jnp.int32, (8, RANK), 1)
+    lane_row = lax.broadcasted_iota(jnp.int32, (1, RANK), 1)
+    for base in range(0, RANK, BLK):
+        end = base + BLK
+        rows = slice(base, end)
+        z, w = eliminate(a_ref[rows, :], lane - base, base // 128, base % 128, 1.0)
+        done = lane_row < end
+        z_ref[rows, :] = jnp.where(done, z, 0.0)
+        w_ref[rows, :] = jnp.where(done, w, 0.0)
+        if end < RANK:
+            left = end // 128 * 128
+            inside = (lane_row >= base) & done
+            update = outer_dot(z[:, left:], w)[end - left :, :]
+            a_ref[end:, :] = jnp.where(inside, 0.0, a_ref[end:, :]) - update
 
 
 def diagonal(gram):
@@ -177,6 +194,8 @@
     gt_v,
     a_v,
     gn_v,
+    zf_v,
+    wf_v,
     g1_v,
     g1x_v,
     g1s_v,
@@ -214,6 +233,7 @@
     tq_v,
     ta_v,
     time_v,
+    relay_sem,
     load_sem,
     send_sem,
     recv_sem,
@@ -252,7 +272,7 @@
         )
         return c
 
-    lax.fori_loop(0, NZ - 1, greet_z, 0)
+    lax.fori_loop(NZ // 2 - 1, NZ - 1, greet_z, 0)
     lax.fori_loop(1, NXS, greet_xs, 0)
 
     waiting = {}
@@ -416,7 +436,12 @@
             rows = slice(xx * 128 + h * 64, xx * 128 + (h + 1) * 64)
             y_v[rows, :] = part[h * 64 : (h + 1) * 64, :] * keep
 
-    pl.semaphore_wait(barrier, NZ - 1 + NXS - 1)
+    pl.semaphore_wait(barrier, NZ // 2 + NXS - 1)
+
+    for step in (NZ // 4, NZ - NZ // 4):
+        pl.semaphore_signal(
+            relay_sem, inc=1, device_id=at((z + step) % NZ, x, src), device_id_type=MESH
+        )
     yield waiting
 
     send_x(g1_v, g1x_v, 0)
@@ -444,6 +469,7 @@
 
     arrived(0)
     g1s_v[...] = (g1x_v[0] + g1x_v[1]) + (g1x_v[2] + g1x_v[3])
+    pl.semaphore_wait(relay_sem, 2)
     corner_z(g1s_v, c1_v, d1_v, c1z_v, d1z_v, 23)
 
     expect(7, yz_v.at[pl.ds(0, NZ - 1)])
@@ -466,11 +492,6 @@
     )
     yield waiting
 
-    def flip(k, c):
-        xt_v[k] = x_v[k].T
-        return c
-
-    lax.fori_loop(0, SAMPLES, flip, 0)
 
     corner_sum(c1s_v, d1s_v, c1z_v, d1z_v, 23)
     corner_xs(c1s_v, d1s_v, c1a_v, d1a_v, 1)
@@ -510,6 +531,12 @@
 
     forward(mine)
     yield waiting
+
+    def flip(k, c):
+        xt_v[k] = x_v[k].T
+        return c
+
+    lax.fori_loop(0, SAMPLES, flip, 0)
 
     forward_group(3)
     forward_group(2)
@@ -620,13 +647,13 @@
     mraw_v[mic_own, :] = mraw_v[mic_own, :] / mic_row
     store_mic = pltpu.make_async_copy(mraw_v.at[mic_own, :], mic_out, load_sem.at[1])
     store_mic.start()
-    invert(a_v)
+    factor(a_v, zf_v, wf_v)
     yield waiting
 
     arrived(22)
     total = ta_v[...].reshape(SAMPLES, RANK)
     total = total / (src_row * mic_row)
-    time_raw = -exact_dot(total, a_v[...])
+    time_raw = exact_dot(exact_dot(total, zf_v[...], ((1,), (1,))), wf_v[...])
     time_diag = jnp.sum(time_raw * time_raw, axis=0, keepdims=True)
     time_v[...] = time_raw / jnp.sqrt(time_diag / SAMPLES + 1e-06)
     store_time = pltpu.make_async_copy(time_v, time_out, load_sem.at[2])
@@ -683,6 +710,8 @@
             pltpu.VMEM((SRC_DEV, RANK), F32),
             pltpu.VMEM((SRC_DEV, RANK), F32),
             pltpu.VMEM((SRC_DEV, RANK), BF16),
+            pltpu.VMEM((RANK, RANK), F32),
+            pltpu.VMEM((RANK, RANK), F32),
             pltpu.VMEM((RANK, RANK), F32),
             pltpu.VMEM((RANK, RANK), F32),
             pltpu.VMEM((RANK, RANK), F32),
@@ -723,6 +752,7 @@
             pltpu.VMEM((1, RANK), F32),
             pltpu.VMEM((NXS, 1, RANK), F32),
             pltpu.VMEM((SAMPLES, RANK), F32),
+            pltpu.SemaphoreType.REGULAR,
             pltpu.SemaphoreType.DMA((4,)),
             pltpu.SemaphoreType.DMA((STAGES,)),
             pltpu.SemaphoreType.DMA((STAGES,)),

time: 99.6 us -> 99.5 us (level)
  no operation moved by 1% of the time
where the time goes in v6:
time: 99.5 us; the launch traced here: 99.4 us
  Pallas kernels  98.7 us (99%)
    pallas_call x1, Pallas kernels, on_device(): pl.pallas_call(functools.partial(kernel, stop=stop), name=name, out_shape...  96.8 us

profile of v6, /device:TPU:1, one launch (start us, length us, event | category | flops | bytes accessed | tf_op | source)
XLA Modules:
  0.0 99.4 jit_solution(17459781266155456051)
XLA Ops:
  0.6 96.8 %shard_map.67 = (f32[512,256]{1,0:T(8,128)}, f32[128,256]{1,0:T(8,128)}, f32[32,256]{1,0:T(8,128)}) custom-call(bf16[32,512,128]{2,1,0:T(8,128)(2,1)} %refs_0_.1, s32[1,8]{1,0:T(1,128)} %bitcast.1, f32[128,256]{1,0:T(8,128)} %refs_2_.1, f32[32,256]{1,0:T(8,128)} %refs_3_.1), custom_call_target="tpu_custom_call" | custom-call | tf_op jit(solution)/shard_map/pallas_call | solution.py:692
  97.4 2.0 %shard_map.68 = (f32[512,256]{1,0:T(8,128)}, f32[128,256]{1,0:T(8,128)}, f32[32,256]{1,0:T(8,128)}) custom-call(f32[512,256]{1,0:T(8,128)} %get-tuple-element.6.src_in, f32[128,256]{1,0:T(8,128)} %get-tuple-element.7.mic_in, f32[32,256]{1,0:T(8,128)} %get-tuple-element.8.time_in), custom_call_target="tpu_custom_call" | custom-call | tf_op jit(solution)/shard_map/pallas_call | solution.py:765

commit v7 on v6

--- a/solution.py
+++ b/solution.py
@@ -127,7 +127,7 @@
             between[i]()
 
 
-def factor(a_ref, z_ref, w_ref):
+def factor(a_ref, z_ref, w_ref, after_first):
     lane = lax.broadcasted_iota(jnp.int32, (8, RANK), 1)
     lane_row = lax.broadcasted_iota(jnp.int32, (1, RANK), 1)
     for base in range(0, RANK, BLK):
@@ -142,6 +142,8 @@
             inside = (lane_row >= base) & done
             update = outer_dot(z[:, left:], w)[end - left :, :]
             a_ref[end:, :] = jnp.where(inside, 0.0, a_ref[end:, :]) - update
+        if base == 0:
+            after_first()
 
 
 def diagonal(gram):
@@ -233,7 +235,6 @@
     tq_v,
     ta_v,
     time_v,
-    relay_sem,
     load_sem,
     send_sem,
     recv_sem,
@@ -272,7 +273,7 @@
         )
         return c
 
-    lax.fori_loop(NZ // 2 - 1, NZ - 1, greet_z, 0)
+    lax.fori_loop(0, NZ - 1, greet_z, 0)
     lax.fori_loop(1, NXS, greet_xs, 0)
 
     waiting = {}
@@ -436,12 +437,7 @@
             rows = slice(xx * 128 + h * 64, xx * 128 + (h + 1) * 64)
             y_v[rows, :] = part[h * 64 : (h + 1) * 64, :] * keep
 
-    pl.semaphore_wait(barrier, NZ // 2 + NXS - 1)
-
-    for step in (NZ // 4, NZ - NZ // 4):
-        pl.semaphore_signal(
-            relay_sem, inc=1, device_id=at((z + step) % NZ, x, src), device_id_type=MESH
-        )
+    pl.semaphore_wait(barrier, NZ - 1 + NXS - 1)
     yield waiting
 
     send_x(g1_v, g1x_v, 0)
@@ -469,7 +465,6 @@
 
     arrived(0)
     g1s_v[...] = (g1x_v[0] + g1x_v[1]) + (g1x_v[2] + g1x_v[3])
-    pl.semaphore_wait(relay_sem, 2)
     corner_z(g1s_v, c1_v, d1_v, c1z_v, d1z_v, 23)
 
     expect(7, yz_v.at[pl.ds(0, NZ - 1)])
@@ -636,18 +631,21 @@
     corner_sum(c3s_v, d3s_v, c3z_v, d3z_v, 25)
     yield waiting
     corner_xs(c3s_v, d3s_v, c3a_v, d3a_v, 18)
-    arrived(21)
-    tq_v[...] = jnp.sum(tz_v[...], axis=0)
-    send_xs(tq_v, ta_v, 22)
     gram_mic = corner_gram(c3a_v, d3a_v, 18)
     yield waiting
 
     mic_row, mic_col = scales_of(gram_mic, MIC_ALL)
     a_v[...] = gn_v[...] * (gram_mic / (mic_row * mic_col)) * (1.0 / (SRC_ALL * MIC_ALL))
-    mraw_v[mic_own, :] = mraw_v[mic_own, :] / mic_row
     store_mic = pltpu.make_async_copy(mraw_v.at[mic_own, :], mic_out, load_sem.at[1])
-    store_mic.start()
-    factor(a_v, zf_v, wf_v)
+
+    def pass_on_time():
+        arrived(21)
+        tq_v[...] = jnp.sum(tz_v[...], axis=0)
+        send_xs(tq_v, ta_v, 22)
+        mraw_v[mic_own, :] = mraw_v[mic_own, :] / mic_row
+        store_mic.start()
+
+    factor(a_v, zf_v, wf_v, pass_on_time)
     yield waiting
 
     arrived(22)
@@ -752,7 +750,6 @@
             pltpu.VMEM((1, RANK), F32),
             pltpu.VMEM((NXS, 1, RANK), F32),
             pltpu.VMEM((SAMPLES, RANK), F32),
-            pltpu.SemaphoreType.REGULAR,
             pltpu.SemaphoreType.DMA((4,)),
             pltpu.SemaphoreType.DMA((STAGES,)),
             pltpu.SemaphoreType.DMA((STAGES,)),

time: 99.5 us -> 102 us (1.025)
  Pallas kernels: 98.7 us -> 101 us
    pallas_call x1, Pallas kernels: 96.8 us -> 99.5 us  [on_device(): pl.pallas_call(functools.partial(kernel, stop=stop), name=name, out_shape...]
where the time goes in v7:
time: 102 us
  Pallas kernels  101 us (99%)
    pallas_call x1, Pallas kernels, on_device(): pl.pallas_call(functools.partial(kernel, stop=stop), name=name, out_shape...  99.5 us

profile of v7, /device:TPU:1, one launch (start us, length us, event | category | flops | bytes accessed | tf_op | source)
XLA Modules:
  0.0 102.1 jit_solution(5323573098089515913)
XLA Ops:
  0.6 99.5 %shard_map.67 = (f32[512,256]{1,0:T(8,128)}, f32[128,256]{1,0:T(8,128)}, f32[32,256]{1,0:T(8,128)}) custom-call(bf16[32,512,128]{2,1,0:T(8,128)(2,1)} %refs_0_.1, s32[1,8]{1,0:T(1,128)} %bitcast.1, f32[128,256]{1,0:T(8,128)} %refs_2_.1, f32[32,256]{1,0:T(8,128)} %refs_3_.1), custom_call_target="tpu_custom_call" | custom-call | tf_op jit(solution)/shard_map/pallas_call | solution.py:690
  100.2 2.0 %shard_map.68 = (f32[512,256]{1,0:T(8,128)}, f32[128,256]{1,0:T(8,128)}, f32[32,256]{1,0:T(8,128)}) custom-call(f32[512,256]{1,0:T(8,128)} %get-tuple-element.6.src_in, f32[128,256]{1,0:T(8,128)} %get-tuple-element.7.mic_in, f32[32,256]{1,0:T(8,128)} %get-tuple-element.8.time_in), custom_call_target="tpu_custom_call" | custom-call | tf_op jit(solution)/shard_map/pallas_call | solution.py:762
